TPU v7x, 32 devices: a whole 2x2x4 slice. The times are simulated.
32 devices in a mesh: group: 2 (over y), row: 4 (over z), col: 2 (over x), depth: 2 (over core).
Axes of the slice: x: 2, y: 2, z: 4, core: 2. Of those that a mesh axis runs over, the one named last changes fastest.
Arguments:
- preact: bfloat16 [1024, 24576], P(('group', 'col', 'depth'), 'row'), parts along dimension 0, may hold values from -6 to 6
- weight: bfloat16 [24576, 6144], P('row', ('col', 'depth')), may hold values from -0.0390625 to 0.0390625
- out_grad: bfloat16 [1024, 6144], P(('group', 'row'), ('col', 'depth')), parts along dimension 0, may hold values from -6 to 6
Outputs:
- preact_grad: bfloat16 [1024, 24576], P(('group', 'col', 'depth'), 'row'), parts along dimension 0
- weight_grad: bfloat16 [49152, 6144], P(('group', 'row'), ('col', 'depth')), parts along dimension 0
There are 2 independent parts, one for each index of `group`. A program takes and returns all parts, laid end to end along the dimension named above; an argument that names none is the same for every part. Nothing has to cross between parts.
All inputs are finite; a program needn't handle non-finite values.
Results may differ from a plain program's by a relative error of at most 0.0047.
Values may be sent and summed in bfloat16 or wider, within the bound.
No kernel may reach another device: no remote copies, remote signals or barrier semaphores. Data moves between devices by JAX's collectives and lax.ppermute only.
A program may use at most 256 MiB of HBM per device.

v0:
```python
import math

import jax
import jax.numpy as jnp
from jax import lax
from jax.sharding import PartitionSpec as P

root_two_pi = 0.7978845608
cubic = 0.044715


def gelu_value(value):
    inner = jnp.tanh(root_two_pi * (value + cubic * value * value * value))
    return 0.5 * value * (1.0 + inner)


def gelu_slope(value):
    inner = jnp.tanh(root_two_pi * (value + cubic * value * value * value))
    return 0.5 * (1.0 + inner) + 0.5 * value * (1.0 - inner * inner) * root_two_pi * (
        1.0 + 3.0 * cubic * value * value
    )


def per_device(preact, weight, out_grad):
    all_grad = lax.all_gather(out_grad, "row", axis=0, tiled=True)
    tokens_all = all_grad.shape[0]
    scale = 1.0 / math.sqrt(tokens_all)
    wide = preact.astype(jnp.float32)
    hidden = gelu_value(
        lax.all_gather(preact, ("col", "depth"), axis=0, tiled=True).astype(jnp.float32)
    ).astype(jnp.bfloat16)
    summed = lax.dot_general(
        hidden, all_grad, (((0,), (0,)), ((), ())), preferred_element_type=jnp.float32
    )
    weight_grad = (summed * scale).astype(jnp.bfloat16)
    own_grad = lax.all_to_all(all_grad, ("col", "depth"), split_axis=0, concat_axis=1, tiled=True)
    hidden_grad = lax.dot_general(
        own_grad,
        lax.all_gather(weight, ("col", "depth"), axis=1, tiled=True),
        (((1,), (1,)), ((), ())),
        preferred_element_type=jnp.float32,
    )
    preact_grad = (hidden_grad * gelu_slope(wide)).astype(jnp.bfloat16)
    return (preact_grad, weight_grad)


def solution(mesh):
    return jax.shard_map(
        per_device,
        mesh=mesh,
        in_specs=(
            P(("group", "col", "depth"), "row"),
            P("row", ("col", "depth")),
            P(("group", "row"), ("col", "depth")),
        ),
        out_specs=(P(("group", "col", "depth"), "row"), P(("group", "row"), ("col", "depth"))),
        check_vma=False,
    )
```

profile of v0, /device:TPU:0, one launch (start us, length us, event | category | flops | bytes accessed | tf_op | source)
XLA Modules:
  0.0 588.9 jit_solution(4037320708200053384)
XLA Ops:
  7.2 0.0 all-gather.4.cloned.1.call-start
  7.2 0.7 all-gather.4.cloned.1.call-update
  7.9 0.0 all-gather.8.cloned.1.call-start
  7.9 0.7 all-gather.8.cloned.1.call-update
  8.6 0.0 all-gather.6.cloned.1.call-start
  8.7 0.7 all-gather.6.cloned.1.call-update
  9.4 40.0 %all-gather.4.cloned.1.call-done = bf16[512,1536]{1,0:T(8,128)(2,1)} async-done(((bf16[128,1536]{1,0:T(8,128)(2,1)}), bf16[512,1536]{1,0:T(8,128)(2,1)}) %all-gather.4.cloned.1.call-update) | async-done | bytes 1572880 | tf_op jit(solution)/shard_map/all_gather | solution.py:25
  49.4 0.0 copy-start.1
  49.4 36.4 %all_to_all.19 = bf16[4,128,1536]{2,1,0:T(8,128)(2,1)S(1)} all-to-all(bf16[4,128,1536]{2,1,0:T(8,128)(2,1)} %bitcast.7), channel_id=1, replica_groups=mesh['group'=2,'row'=4,'col'=2,'depth'=2] {'col','depth'}, dimensions={0} | all-to-all | bytes 3145728 | tf_op jit(solution)/shard_map/all_to_all | solution.py:36
  85.8 1.6 copy.5
  87.3 0.0 copy-start
  87.4 21.2 %all-gather.8.cloned.1.call-done = bf16[512,6144]{1,0:T(8,128)(2,1)} async-done(((bf16[128,6144]{1,0:T(8,128)(2,1)}), bf16[512,6144]{1,0:T(8,128)(2,1)}) %all-gather.8.cloned.1.call-update) | async-done | bytes 6291472 | tf_op jit(solution)/shard_map/all_gather | solution.py:30
  108.5 0.0 copy-done.1
  108.5 24.6 %multiply_convert_fusion = bf16[6144,1536]{1,0:T(8,128)(2,1)} fusion(bf16[512,1536]{1,0:T(8,128)(2,1)S(1)} %copy-done.1, bf16[512,6144]{1,0:T(8,128)(2,1)} %all-gather.8.cloned.1.call-done), kind=kOutput, calls=%fused_computation | convolution fusion | flops 9714008064 | bytes 26738688 | tf_op jit(solution)/shard_map/dot_general | solution.py:32
  133.2 416.5 %all-gather.6.cloned.1.call-done = bf16[6144,6144]{1,0:T(8,128)(2,1)} async-done(((bf16[6144,1536]{1,0:T(8,128)(2,1)}), bf16[6144,6144]{1,0:T(8,128)(2,1)}) %all-gather.6.cloned.1.call-update) | async-done | bytes 75497488 | tf_op jit(solution)/shard_map/all_gather | solution.py:39
  549.7 0.0 copy-done
  549.7 32.7 %fusion.5 = bf16[128,6144]{1,0:T(8,128)(2,1)} fusion(bf16[128,6144]{0,1:T(8,128)(2,1)} %bitcast.8, bf16[6144,6144]{1,0:T(8,128)(2,1)} %all-gather.6.cloned.1.call-done, bf16[128,6144]{1,0:T(8,128)(2,1)S(1)} %copy-done), kind=kOutput, calls=%fused_computation.19 | convolution fusion | flops 9679405056 | bytes 80216064 | tf_op jit(solution)/shard_map/dot_general | solution.py:37
Async XLA Ops:
  7.2 42.2 %all-gather.4.cloned.1.call-start = ((), (), s32[]{:S(2)}) async-start(), calls=%async_computation.1 | async-start | bytes 1966080 | tf_op jit(solution)/shard_map/all_gather | solution.py:25
  7.9 100.6 %all-gather.8.cloned.1.call-start = ((), (), s32[]{:S(2)}) async-start(), calls=%async_computation.3 | async-start | bytes 7864320 | tf_op jit(solution)/shard_map/all_gather | solution.py:30
  8.6 541.0 %all-gather.6.cloned.1.call-start = ((), (), s32[]{:S(2)}) async-start(), calls=%async_computation.2 | async-start | bytes 94371840 | tf_op jit(solution)/shard_map/all_gather | solution.py:39
  49.4 59.1 %copy-start.1 = (bf16[512,1536]{1,0:T(8,128)(2,1)S(1)}, bf16[512,1536]{1,0:T(8,128)(2,1)}, u32[]{:S(2)}) copy-start(bf16[512,1536]{1,0:T(8,128)(2,1)} %all-gather.4.cloned.1.call-done) | copy-start | bytes 4718596
  87.3 462.3 %copy-start = (bf16[128,6144]{1,0:T(8,128)(2,1)S(1)}, bf16[128,6144]{1,0:T(8,128)(2,1)}, u32[]{:S(2)}) copy-start(bf16[128,6144]{1,0:T(8,128)(2,1)} %param.3) | copy-start | bytes 4718596
Sparse Core Ops, SparseCore 0:
  9.6 39.7 all-gather.3
  51.0 57.5 all-gather.7
  110.1 439.4 all-gather.5
where the time goes:
time: 589 us
  waiting for transfers between devices  480 us (81%)
  matrix products  57.3 us (10%)
  blocking collectives  36.4 us (6%)
  between operations  13.7 us (2%)
    all_gather x1, waiting for transfers between devices, per_device(): lax.all_gather(weight, ('col', 'depth'), axis=1, tiled=True)  416 us
    all_gather x1, waiting for transfers between devices, per_device(): all_grad = lax.all_gather(out_grad, 'row', axis=0, tiled=True)  40 us
    all_to_all x1, blocking collectives, per_device(): lax.all_to_all(all_grad, ('col', 'depth'), split_axis=0, concat_axis=1, t...  36.4 us
    dot_general x1, matrix products, per_device(): lax.dot_general(own_grad, lax.all_gather(weight, ('col', 'depth'), axis=1...  32.7 us
    dot_general x1, matrix products, per_device(): lax.dot_general(hidden, all_grad, (((0,), (0,)), ((), ())), preferred_ele...  24.6 us
    all_gather x1, waiting for transfers between devices, per_device(): lax.all_gather(preact, ('col', 'depth'), axis=0, tiled=True)  21.2 us
  transfers between devices with their start and end apart: 3, of which 3 were waited for; matrix products, arithmetic and copies ran while one was open for 4% of the time, Pallas kernels for 0%

commit v1 on v0

v1 whole, which is shorter than its diff:
```python
import math

import jax
import jax.numpy as jnp
from jax import lax
from jax.sharding import PartitionSpec as P

root_two_pi = 0.7978845608
cubic = 0.044715
f32 = jnp.float32
bf16 = jnp.bfloat16

HIDDEN_CHUNKS = 4
PARTIAL_CHUNKS = 4


def gelu_value(value):
    inner = jnp.tanh(root_two_pi * (value + cubic * value * value * value))
    return 0.5 * value * (1.0 + inner)


def gelu_slope(value):
    inner = jnp.tanh(root_two_pi * (value + cubic * value * value * value))
    return 0.5 * (1.0 + inner) + 0.5 * value * (1.0 - inner * inner) * root_two_pi * (
        1.0 + 3.0 * cubic * value * value
    )


def to_next(array, axis, size, hop):
    return lax.ppermute(array, axis, [(i, (i + hop) % size) for i in range(size)])


def from_next(array, axis, size, hop):
    return lax.ppermute(array, axis, [((i + hop) % size, i) for i in range(size)])


def solution(mesh):
    rows, cols, depths = mesh.shape["row"], mesh.shape["col"], mesh.shape["depth"]

    def row_blocks(out_grad):
        if rows > 4:
            whole = lax.all_gather(out_grad, "row", axis=0, tiled=False)
            own = lax.axis_index("row")
            return [
                lax.dynamic_index_in_dim(whole, lax.rem(own - s + rows, rows), 0, False)
                for s in range(rows)
            ]
        blocks = [out_grad]
        for _ in range(rows - 1):
            blocks.append(to_next(blocks[-1], "row", rows, 1))
        return blocks

    def per_device(preact, weight, out_grad):
        block, features = preact.shape
        row_tokens, width = out_grad.shape
        tokens = row_tokens * rows
        scale = 1.0 / math.sqrt(tokens)
        x, d, z = lax.axis_index("col"), lax.axis_index("depth"), lax.axis_index("row")

        stack = jnp.stack(row_blocks(out_grad))
        per_block = block // row_tokens
        ordered = []
        for dd in range(depths):
            for dx in range(cols):
                owner = lax.rem(x + dx, cols) * depths + lax.rem(d + dd, depths)
                for part in range(per_block):
                    place = lax.rem(z - (owner * per_block + part) + rows, rows)
                    ordered.append(lax.dynamic_index_in_dim(stack, place, 0, False))
        grads = jnp.concatenate(ordered, axis=0)
        half = cols * block

        wide = features // HIDDEN_CHUNKS
        hidden = []
        for c in range(HIDDEN_CHUNKS):
            own = gelu_value(preact[:, c * wide : (c + 1) * wide].astype(f32)).astype(bf16)
            mine = [own] + [from_next(own, "col", cols, dx) for dx in range(1, cols)]
            mine = jnp.concatenate(mine, axis=0)
            both = [mine] + [from_next(mine, "depth", depths, dd) for dd in range(1, depths)]
            hidden.append(jnp.concatenate(both, axis=0))

        wide = features // PARTIAL_CHUNKS
        pieces = []
        for c in range(PARTIAL_CHUNKS):
            rows_of = weight[c * wide : (c + 1) * wide]
            part = lax.dot_general(
                grads, rows_of, (((1,), (1,)), ((), ())), preferred_element_type=f32
            )
            total = part[:half]
            for dd in range(1, depths):
                sent = part[dd * half : (dd + 1) * half].astype(bf16)
                total = total + to_next(sent, "depth", depths, dd).astype(f32)
            mine = total[:block]
            for dx in range(1, cols):
                sent = total[dx * block : (dx + 1) * block].astype(bf16)
                mine = mine + to_next(sent, "col", cols, dx).astype(f32)
            value = preact[:, c * wide : (c + 1) * wide].astype(f32)
            pieces.append((mine * gelu_slope(value)).astype(bf16))
        preact_grad = jnp.concatenate(pieces, axis=1)

        weight_grad = []
        for part in hidden:
            summed = lax.dot_general(
                part, grads, (((0,), (0,)), ((), ())), preferred_element_type=f32
            )
            weight_grad.append((summed * scale).astype(bf16))
        return preact_grad, jnp.concatenate(weight_grad, axis=0)

    return jax.shard_map(
        per_device,
        mesh=mesh,
        in_specs=(
            P(("group", "col", "depth"), "row"),
            P("row", ("col", "depth")),
            P(("group", "row"), ("col", "depth")),
        ),
        out_specs=(P(("group", "col", "depth"), "row"), P(("group", "row"), ("col", "depth"))),
        check_vma=False,
    )
```

time: 589 us -> 191 us (0.32)
  waiting for transfers between devices: 480 us -> 95.9 us
  other arithmetic: 0 us -> 48.8 us
  blocking collectives: 36.4 us -> 0 us
  matrix products: 57.3 us -> 30.5 us
  starting transfers between devices: 0.11 us -> 13.6 us
  between operations: 13.7 us -> 0.88 us
    all_gather x3 -> x0, waiting for transfers between devices: 478 us -> none  [the longest x1 416 us: per_device(): lax.all_gather(weight, ('col', 'depth'), axis=1, tiled=True)]
    ppermute x0 -> x19, waiting for transfers between devices: none -> 95.9 us  [the longest x11 65.9 us: to_next(): lax.ppermute(array, axis, [(i, (i + hop) % size) for i in range(size)])]
    concatenate x0 -> x6, other arithmetic: none -> 44.3 us  [the longest x1 42.8 us: per_device(): return (preact_grad, jnp.concatenate(weight_grad, axis=0))]
    all_to_all x1 -> x0, blocking collectives: 36.4 us -> none  [per_device(): lax.all_to_all(all_grad, ('col', 'depth'), split_axis=0, concat_axis=1, t...]
    dot_general x2 -> x8, matrix products: 57.3 us -> 30.5 us  [the longest x4 19.9 us: per_device(): lax.dot_general(grads, rows_of, (((1,), (1,)), ((), ())), preferred_eleme...]
    ppermute x0 -> x19, starting transfers between devices: none -> 13.6 us  [the longest x11 8.66 us: to_next(): lax.ppermute(array, axis, [(i, (i + hop) % size) for i in range(size)])]
  transfers between devices with their start and end apart: 3 -> 19, of which waited for: 3 -> 9; matrix products, arithmetic and copies ran while one was open for 4% -> 11% of each run, Pallas kernels for 0% -> 0%
where the time goes in v1:
time: 191 us; the launch traced here: 190 us
  waiting for transfers between devices  95.9 us (50%)
  other arithmetic  48.8 us (26%)
  matrix products  30.5 us (16%)
  starting transfers between devices  13.6 us (7%)
    ppermute x11, waiting for transfers between devices, to_next(): lax.ppermute(array, axis, [(i, (i + hop) % size) for i in range(size)])  65.9 us
    concatenate x1, other arithmetic, per_device(): return (preact_grad, jnp.concatenate(weight_grad, axis=0))  42.8 us
    ppermute x8, waiting for transfers between devices, from_next(): lax.ppermute(array, axis, [((i + hop) % size, i) for i in range(size)])  30 us
    dot_general x4, matrix products, per_device(): lax.dot_general(grads, rows_of, (((1,), (1,)), ((), ())), preferred_eleme...  19.9 us
    dot_general x4, matrix products, per_device(): lax.dot_general(part, grads, (((0,), (0,)), ((), ())), preferred_element_...  10.6 us
    ppermute x11, starting transfers between devices, to_next(): lax.ppermute(array, axis, [(i, (i + hop) % size) for i in range(size)])  8.66 us
    ppermute x8, starting transfers between devices, from_next(): lax.ppermute(array, axis, [((i + hop) % size, i) for i in range(size)])  4.91 us
  transfers between devices with their start and end apart: 19, of which 9 were waited for; matrix products, arithmetic and copies ran while one was open for 11% of the time, Pallas kernels for 0%

profile of v1, /device:TPU:0, one launch (start us, length us, event | category | flops | bytes accessed | tf_op | source)
XLA Modules:
  0.0 190.3 jit_solution(9471485867475629389)
XLA Ops:
  0.6 3.1 %collective-permute-start = (bf16[128,1536]{1,0:T(8,128)(2,1)}, bf16[128,1536]{1,0:T(8,128)(2,1)S(1)}, u32[]{:S(2)}, u32[]{:S(2)}) collective-permute-start(bf16[128,1536]{1,0:T(8,128)(2,1)} %param.5), channel_id=1, source_target_pairs={{0,4},{4,8},{8,12},{12,0},{1,5},{5,9},{9,13},{13,1},{2,6},{6,10},{... | collective-permute-start | bytes 1179656 | tf_op jit(solution)/shard_map/ppermute | solution.py:30
  3.7 11.3 %collective-permute-done = bf16[128,1536]{1,0:T(8,128)(2,1)S(1)} collective-permute-done((bf16[128,1536]{1,0:T(8,128)(2,1)}, bf16[128,1536]{1,0:T(8,128)(2,1)S(1)}, u32[]{:S(2)}, u32[]{:S(2)}) %collective-permute-start) | collective-permute-done | bytes 393248 | tf_op jit(solution)/shard_map/ppermute | solution.py:30
  15.1 0.0 collective-permute-start.1
  15.1 12.1 %collective-permute-done.1 = bf16[128,1536]{1,0:T(8,128)(2,1)S(1)} collective-permute-done((bf16[128,1536]{1,0:T(8,128)(2,1)S(1)}, bf16[128,1536]{1,0:T(8,128)(2,1)S(1)}, u32[]{:S(2)}, u32[]{:S(2)}) %collective-permute-start.1) | collective-permute-done | bytes 393248 | tf_op jit(solution)/shard_map/ppermute | solution.py:30
  27.2 0.0 collective-permute-start.2
  27.2 11.2 %collective-permute-done.2 = bf16[128,1536]{1,0:T(8,128)(2,1)S(1)} collective-permute-done((bf16[128,1536]{1,0:T(8,128)(2,1)S(1)}, bf16[128,1536]{1,0:T(8,128)(2,1)S(1)}, u32[]{:S(2)}, u32[]{:S(2)}) %collective-permute-start.2) | collective-permute-done | bytes 393248 | tf_op jit(solution)/shard_map/ppermute | solution.py:30
  38.3 1.2 pad_maximum_fusion.1
  39.5 0.1 dynamic-slice_bitcast_fusion.3
  39.7 5.0 %fusion.8 = f32[512,1536]{1,0:T(8,128)S(1)} fusion(bf16[6144,1536]{1,0:T(8,128)(2,1)} %param.4, bf16[128,1536]{1,0:T(8,128)(2,1)S(1)} %get-tuple-element.11, bf16[128,1536]{1,0:T(8,128)(2,1)S(1)} %get-tuple-element.12, bf16[128,1536]{1,0:T(8,128)(2,1)S(1)} %get-tuple-element.13, bf16[128,1536]{1,0:T(8,128)(2,1)S(1)} %get-tuple-element.10), kind=kOutput, calls=%fused_computation.13 | convolution fusion | flops 2422210560 | bytes 9437184 | tf_op jit(solution)/shard_map/dot_general | solution.py:85
  44.6 5.0 %fusion.6 = f32[512,1536]{1,0:T(8,128)S(1)} fusion(bf16[6144,1536]{1,0:T(8,128)(2,1)} %param.4, bf16[128,1536]{1,0:T(8,128)(2,1)S(1)} %get-tuple-element.11, bf16[128,1536]{1,0:T(8,128)(2,1)S(1)} %get-tuple-element.12, bf16[128,1536]{1,0:T(8,128)(2,1)S(1)} %get-tuple-element.13, bf16[128,1536]{1,0:T(8,128)(2,1)S(1)} %get-tuple-element.10), kind=kOutput, calls=%fused_computation.11 | convolution fusion | flops 2422210560 | bytes 9437184 | tf_op jit(solution)/shard_map/dot_general | solution.py:85
  49.6 0.1 slice.166
  49.7 0.1 collective-permute-start.5
  49.8 5.0 %fusion.4 = f32[512,1536]{1,0:T(8,128)S(1)} fusion(bf16[6144,1536]{1,0:T(8,128)(2,1)} %param.4, bf16[128,1536]{1,0:T(8,128)(2,1)S(1)} %get-tuple-element.11, bf16[128,1536]{1,0:T(8,128)(2,1)S(1)} %get-tuple-element.12, bf16[128,1536]{1,0:T(8,128)(2,1)S(1)} %get-tuple-element.13, bf16[128,1536]{1,0:T(8,128)(2,1)S(1)} %get-tuple-element.10), kind=kOutput, calls=%fused_computation.9 | convolution fusion | flops 2422210560 | bytes 9437184 | tf_op jit(solution)/shard_map/dot_general | solution.py:85
  54.7 0.1 slice.165
  54.8 0.6 collective-permute-start.7
  55.4 5.0 %fusion.10 = f32[512,1536]{1,0:T(8,128)S(1)} fusion(bf16[6144,1536]{1,0:T(8,128)(2,1)} %param.4, bf16[128,1536]{1,0:T(8,128)(2,1)S(1)} %get-tuple-element.11, bf16[128,1536]{1,0:T(8,128)(2,1)S(1)} %get-tuple-element.12, bf16[128,1536]{1,0:T(8,128)(2,1)S(1)} %get-tuple-element.13, bf16[128,1536]{1,0:T(8,128)(2,1)S(1)} %get-tuple-element.10), kind=kOutput, calls=%fused_computation.15 | convolution fusion | flops 2422210560 | bytes 9437184 | tf_op jit(solution)/shard_map/dot_general | solution.py:85
  60.3 0.1 slice.164
  60.4 0.1 collective-permute-start.9
  60.5 0.1 slice.167
  60.6 0.6 collective-permute-start.3
  61.2 0.0 collective-permute-done.5
  61.2 0.2 slice_add_fusion.2
  61.4 1.1 collective-permute-start.6
  62.5 0.0 collective-permute-done.7
  62.5 0.2 slice_add_fusion.1
  62.7 1.1 collective-permute-start.8
  63.8 0.0 collective-permute-done.9
  63.8 0.2 slice_add_fusion
  64.0 0.0 copy-start
  64.1 1.1 collective-permute-start.10
  65.2 0.0 collective-permute-done.3
  65.2 0.2 slice_add_fusion.3
  65.4 1.1 collective-permute-start.4
  66.5 6.9 %collective-permute-done.6 = bf16[128,1536]{1,0:T(8,128)(2,1)S(1)} collective-permute-done((bf16[128,1536]{1,0:T(8,128)(2,1)S(1)}, bf16[128,1536]{1,0:T(8,128)(2,1)S(1)}, u32[]{:S(2)}, u32[]{:S(2)}) %collective-permute-start.6) | collective-permute-done | bytes 393248 | tf_op jit(solution)/shard_map/ppermute | solution.py:30
  73.5 8.4 %collective-permute-done.8 = bf16[128,1536]{1,0:T(8,128)(2,1)S(1)} collective-permute-done((bf16[128,1536]{1,0:T(8,128)(2,1)S(1)}, bf16[128,1536]{1,0:T(8,128)(2,1)S(1)}, u32[]{:S(2)}, u32[]{:S(2)}) %collective-permute-start.8) | collective-permute-done | bytes 393248 | tf_op jit(solution)/shard_map/ppermute | solution.py:30
  81.9 8.4 %collective-permute-done.10 = bf16[128,1536]{1,0:T(8,128)(2,1)S(1)} collective-permute-done((bf16[128,1536]{1,0:T(8,128)(2,1)S(1)}, bf16[128,1536]{1,0:T(8,128)(2,1)S(1)}, u32[]{:S(2)}, u32[]{:S(2)}) %collective-permute-start.10) | collective-permute-done | bytes 393248 | tf_op jit(solution)/shard_map/ppermute | solution.py:30
  90.3 7.5 %collective-permute-done.4 = bf16[128,1536]{1,0:T(8,128)(2,1)S(1)} collective-permute-done((bf16[128,1536]{1,0:T(8,128)(2,1)S(1)}, bf16[128,1536]{1,0:T(8,128)(2,1)S(1)}, u32[]{:S(2)}, u32[]{:S(2)}) %collective-permute-start.4) | collective-permute-done | bytes 393248 | tf_op jit(solution)/shard_map/ppermute | solution.py:30
  97.8 2.5 %fusion.63 = (bf16[128,1536]{1,0:T(8,128)(2,1)S(1)}, bf16[128,1536]{1,0:T(8,128)(2,1)S(1)}, bf16[128,1536]{1,0:T(8,128)(2,1)S(1)}, bf16[128,1536]{1,0:T(8,128)(2...) fusion(bf16[128,6144]{1,0:T(8,128)(2,1)S(1)} %copy-done, ...), kind=kLoop, calls=%fused_computation.107 | loop fusion | flops 18874368 | bytes 9437184 | tf_op jit(solution)/shard_map/convert_element_type | solution.py:75
  100.3 1.1 collective-permute-start.17
  101.4 1.0 collective-permute-start.11
  102.5 1.0 collective-permute-start.13
  103.5 1.0 collective-permute-start.15
  104.5 8.0 %collective-permute-done.17 = bf16[128,1536]{1,0:T(8,128)(2,1)S(1)} collective-permute-done((bf16[128,1536]{1,0:T(8,128)(2,1)S(1)}, bf16[128,1536]{1,0:T(8,128)(2,1)S(1)}, u32[]{:S(2)}, u32[]{:S(2)}) %collective-permute-start.17) | collective-permute-done | bytes 393248 | tf_op jit(solution)/shard_map/ppermute | solution.py:34
  112.5 0.1 pad_maximum_fusion.7
  112.5 0.1 collective-permute-start.18
  112.6 1.3 pad_maximum_fusion.3
  113.9 22.0 %collective-permute-done.15 = bf16[128,1536]{1,0:T(8,128)(2,1)S(1)} collective-permute-done((bf16[128,1536]{1,0:T(8,128)(2,1)S(1)}, bf16[128,1536]{1,0:T(8,128)(2,1)S(1)}, u32[]{:S(2)}, u32[]{:S(2)}) %collective-permute-start.15) | collective-permute-done | bytes 393248 | tf_op jit(solution)/shard_map/ppermute | solution.py:34
  135.9 0.1 pad_maximum_fusion.6
  135.9 0.1 collective-permute-start.16
  136.0 0.0 collective-permute-done.11
  136.0 0.1 pad_maximum_fusion.4
  136.1 0.5 collective-permute-start.12
  136.6 0.0 collective-permute-done.13
  136.7 0.1 pad_maximum_fusion.5
  136.7 0.1 collective-permute-start.14
  136.8 0.0 collective-permute-done.18
  136.8 2.6 %fusion.3 = bf16[1536,1536]{1,0:T(8,128)(2,1)S(1)} fusion(bf16[256,1536]{1,0:T(8,128)(2,1)S(1)} %collective-permute-done.18, bf16[128,1536]{1,0:T(8,128)(2,1)S(1)} %collective-permute-done.17, bf16[128,1536]{1,0:T(8,128)(2,1)S(1)} %get-tuple-element.5, bf16[128,1536]{1,0:T(8,128)(2,1)S(1)} %get-tuple-element.11, ...), kind=kOutput, calls=%fused_computation.8 | convolution fusion | flops 2431647744 | bytes 7864320 | tf_op jit(solution)/shard_map/dot_general | solution.py:102
  139.5 0.0 collective-permute-done.16
  139.5 2.7 %fusion.2 = bf16[1536,1536]{1,0:T(8,128)(2,1)S(1)} fusion(bf16[256,1536]{1,0:T(8,128)(2,1)S(1)} %collective-permute-done.16, bf16[128,1536]{1,0:T(8,128)(2,1)S(1)} %collective-permute-done.15, bf16[128,1536]{1,0:T(8,128)(2,1)S(1)} %get-tuple-element.4, bf16[128,1536]{1,0:T(8,128)(2,1)S(1)} %get-tuple-element.11, ...), kind=kOutput, calls=%fused_computation.7 | convolution fusion | flops 2431647744 | bytes 7864320 | tf_op jit(solution)/shard_map/dot_general | solution.py:102
  142.1 0.0 collective-permute-done.14
  142.1 2.7 %fusion.1 = bf16[1536,1536]{1,0:T(8,128)(2,1)S(1)} fusion(bf16[256,1536]{1,0:T(8,128)(2,1)S(1)} %collective-permute-done.14, bf16[128,1536]{1,0:T(8,128)(2,1)S(1)} %collective-permute-done.13, bf16[128,1536]{1,0:T(8,128)(2,1)S(1)} %get-tuple-element.3, bf16[128,1536]{1,0:T(8,128)(2,1)S(1)} %get-tuple-element.11, ...), kind=kOutput, calls=%fused_computation.6 | convolution fusion | flops 2431647744 | bytes 7864320 | tf_op jit(solution)/shard_map/dot_general | solution.py:102
  144.8 0.0 collective-permute-done.12
  144.8 2.7 %fusion = bf16[1536,1536]{1,0:T(8,128)(2,1)S(1)} fusion(bf16[256,1536]{1,0:T(8,128)(2,1)S(1)} %collective-permute-done.12, bf16[128,1536]{1,0:T(8,128)(2,1)S(1)} %collective-permute-done.11, bf16[128,1536]{1,0:T(8,128)(2,1)S(1)} %get-tuple-element.2, bf16[128,1536]{1,0:T(8,128)(2,1)S(1)} %get-tuple-element.11, bf16[128,1536]{1,0:T(8,128)(2,1)S(1)} %get-tuple-element.12, ...), kind=kOutput, calls=%fused_computation.5 | convolution fusion | flops 2431647744 | bytes 7864320 | tf_op jit(solution)/shard_map/dot_general | solution.py:102
  147.5 42.8 %pad_maximum_fusion = bf16[6144,1536]{1,0:T(8,128)(2,1)} fusion(bf16[1536,1536]{1,0:T(8,128)(2,1)S(1)} %fusion.3, bf16[1536,1536]{1,0:T(8,128)(2,1)S(1)} %fusion.2, bf16[1536,1536]{1,0:T(8,128)(2,1)S(1)} %fusion.1, bf16[1536,1536]{1,0:T(8,128)(2,1)S(1)} %fusion), kind=kLoop, calls=%fused_computation | loop fusion | flops 75497472 | bytes 37748736 | tf_op jit(solution)/shard_map/concatenate | solution.py:106
  (5 shorter events, 0.2 us)
Async XLA Ops:
  0.6 14.4 %collective-permute-start = (bf16[128,1536]{1,0:T(8,128)(2,1)}, bf16[128,1536]{1,0:T(8,128)(2,1)S(1)}, u32[]{:S(2)}, u32[]{:S(2)}) collective-permute-start(bf16[128,1536]{1,0:T(8,128)(2,1)} %param.5), channel_id=1, source_target_pairs={{0,4},{4,8},{8,12},{12,0},{1,5},{5,9},{9,13},{13,1},{2,6},{6,10},{... | collective-permute-start | bytes 1179656 | tf_op jit(solution)/shard_map/ppermute | solution.py:30
  15.1 12.1 %collective-permute-start.1 = (bf16[128,1536]{1,0:T(8,128)(2,1)S(1)}, bf16[128,1536]{1,0:T(8,128)(2,1)S(1)}, u32[]{:S(2)}, u32[]{:S(2)}) collective-permute-start(bf16[128,1536]{1,0:T(8,128)(2,1)S(1)} %collective-permute-done), channel_id=1, source_target_pairs={{0,4},{4,8},{8,12},{12,0},{1,5},{5,9},{9,13},{13,1},{2,6},{6,10},{... | collective-permute-start | bytes 1179656 | tf_op jit(solution)/shard_map/ppermute | solution.py:30
  27.2 11.2 %collective-permute-start.2 = (bf16[128,1536]{1,0:T(8,128)(2,1)S(1)}, bf16[128,1536]{1,0:T(8,128)(2,1)S(1)}, u32[]{:S(2)}, u32[]{:S(2)}) collective-permute-start(bf16[128,1536]{1,0:T(8,128)(2,1)S(1)} %collective-permute-done.1), channel_id=1, source_target_pairs={{0,4},{4,8},{8,12},{12,0},{1,5},{5,9},{9,13},{13,1},{2,6},{6,10},{... | collective-permute-start | bytes 1179656 | tf_op jit(solution)/shard_map/ppermute | solution.py:30
  49.7 11.5 %collective-permute-start.5 = (bf16[256,1536]{1,0:T(8,128)(2,1)S(1)}, bf16[256,1536]{1,0:T(8,128)(2,1)S(1)}, u32[]{:S(2)}, u32[]{:S(2)}) collective-permute-start(bf16[256,1536]{1,0:T(8,128)(2,1)S(1)} %slice.166), channel_id=1, source_target_pairs={{0,1},{1,0},{2,3},{3,2},{4,5},{5,4},{6,7},{7,6},{8,9},{9,8},{10,11... | collective-permute-start | bytes 2359304 | tf_op jit(solution)/shard_map/ppermute | solution.py:30
  54.8 7.7 %collective-permute-start.7 = (bf16[256,1536]{1,0:T(8,128)(2,1)S(1)}, bf16[256,1536]{1,0:T(8,128)(2,1)S(1)}, u32[]{:S(2)}, u32[]{:S(2)}) collective-permute-start(bf16[256,1536]{1,0:T(8,128)(2,1)S(1)} %slice.165), channel_id=1, source_target_pairs={{0,1},{1,0},{2,3},{3,2},{4,5},{5,4},{6,7},{7,6},{8,9},{9,8},{10,11... | collective-permute-start | bytes 2359304 | tf_op jit(solution)/shard_map/ppermute | solution.py:30
  60.4 3.4 %collective-permute-start.9 = (bf16[256,1536]{1,0:T(8,128)(2,1)S(1)}, bf16[256,1536]{1,0:T(8,128)(2,1)S(1)}, u32[]{:S(2)}, u32[]{:S(2)}) collective-permute-start(bf16[256,1536]{1,0:T(8,128)(2,1)S(1)} %slice.164), channel_id=1, source_target_pairs={{0,1},{1,0},{2,3},{3,2},{4,5},{5,4},{6,7},{7,6},{8,9},{9,8},{10,11... | collective-permute-start | bytes 2359304 | tf_op jit(solution)/shard_map/ppermute | solution.py:30
  60.6 4.5 %collective-permute-start.3 = (bf16[256,1536]{1,0:T(8,128)(2,1)S(1)}, bf16[256,1536]{1,0:T(8,128)(2,1)S(1)}, u32[]{:S(2)}, u32[]{:S(2)}) collective-permute-start(bf16[256,1536]{1,0:T(8,128)(2,1)S(1)} %slice.167), channel_id=1, source_target_pairs={{0,1},{1,0},{2,3},{3,2},{4,5},{5,4},{6,7},{7,6},{8,9},{9,8},{10,11... | collective-permute-start | bytes 2359304 | tf_op jit(solution)/shard_map/ppermute | solution.py:30
  61.4 12.0 %collective-permute-start.6 = (bf16[128,1536]{1,0:T(8,128)(2,1)S(1)}, bf16[128,1536]{1,0:T(8,128)(2,1)S(1)}, u32[]{:S(2)}, u32[]{:S(2)}) collective-permute-start(bf16[128,1536]{1,0:T(8,128)(2,1)S(1)} %slice.170), channel_id=1, source_target_pairs={{0,2},{2,0},{1,3},{3,1},{4,6},{6,4},{5,7},{7,5},{8,10},{10,8},{9,1... | collective-permute-start | bytes 1179656 | tf_op jit(solution)/shard_map/ppermute | solution.py:30
  62.7 19.2 %collective-permute-start.8 = (bf16[128,1536]{1,0:T(8,128)(2,1)S(1)}, bf16[128,1536]{1,0:T(8,128)(2,1)S(1)}, u32[]{:S(2)}, u32[]{:S(2)}) collective-permute-start(bf16[128,1536]{1,0:T(8,128)(2,1)S(1)} %slice.169), channel_id=1, source_target_pairs={{0,2},{2,0},{1,3},{3,1},{4,6},{6,4},{5,7},{7,5},{8,10},{10,8},{9,1... | collective-permute-start | bytes 1179656 | tf_op jit(solution)/shard_map/ppermute | solution.py:30
  64.0 33.8 %copy-start = (bf16[128,6144]{1,0:T(8,128)(2,1)S(1)}, bf16[128,6144]{1,0:T(8,128)(2,1)}, u32[]{:S(2)}) copy-start(bf16[128,6144]{1,0:T(8,128)(2,1)} %param.3) | copy-start | bytes 4718596
  64.1 26.2 %collective-permute-start.10 = (bf16[128,1536]{1,0:T(8,128)(2,1)S(1)}, bf16[128,1536]{1,0:T(8,128)(2,1)S(1)}, u32[]{:S(2)}, u32[]{:S(2)}) collective-permute-start(bf16[128,1536]{1,0:T(8,128)(2,1)S(1)} %slice.168), channel_id=1, source_target_pairs={{0,2},{2,0},{1,3},{3,1},{4,6},{6,4},{5,7},{7,5},{8,10},{10,8},{9,1... | collective-permute-start | bytes 1179656 | tf_op jit(solution)/shard_map/ppermute | solution.py:30
  65.4 32.4 %collective-permute-start.4 = (bf16[128,1536]{1,0:T(8,128)(2,1)S(1)}, bf16[128,1536]{1,0:T(8,128)(2,1)S(1)}, u32[]{:S(2)}, u32[]{:S(2)}) collective-permute-start(bf16[128,1536]{1,0:T(8,128)(2,1)S(1)} %slice.171), channel_id=1, source_target_pairs={{0,2},{2,0},{1,3},{3,1},{4,6},{6,4},{5,7},{7,5},{8,10},{10,8},{9,1... | collective-permute-start | bytes 1179656 | tf_op jit(solution)/shard_map/ppermute | solution.py:30
  100.3 12.1 %collective-permute-start.17 = (bf16[128,1536]{1,0:T(8,128)(2,1)S(1)}, bf16[128,1536]{1,0:T(8,128)(2,1)S(1)}, u32[]{:S(2)}, u32[]{:S(2)}) collective-permute-start(bf16[128,1536]{1,0:T(8,128)(2,1)S(1)} %get-tuple-element.5), channel_id=1, source_target_pairs={{2,0},{0,2},{3,1},{1,3},{6,4},{4,6},{7,5},{5,7},{10,8},{8,10},{11,... | collective-permute-start | bytes 1179656 | tf_op jit(solution)/shard_map/ppermute | solution.py:34
  101.4 34.6 %collective-permute-start.11 = (bf16[128,1536]{1,0:T(8,128)(2,1)S(1)}, bf16[128,1536]{1,0:T(8,128)(2,1)S(1)}, u32[]{:S(2)}, u32[]{:S(2)}) collective-permute-start(bf16[128,1536]{1,0:T(8,128)(2,1)S(1)} %get-tuple-element.2), channel_id=1, source_target_pairs={{2,0},{0,2},{3,1},{1,3},{6,4},{4,6},{7,5},{5,7},{10,8},{8,10},{11,... | collective-permute-start | bytes 1179656 | tf_op jit(solution)/shard_map/ppermute | solution.py:34
  102.5 34.2 %collective-permute-start.13 = (bf16[128,1536]{1,0:T(8,128)(2,1)S(1)}, bf16[128,1536]{1,0:T(8,128)(2,1)S(1)}, u32[]{:S(2)}, u32[]{:S(2)}) collective-permute-start(bf16[128,1536]{1,0:T(8,128)(2,1)S(1)} %get-tuple-element.3), channel_id=1, source_target_pairs={{2,0},{0,2},{3,1},{1,3},{6,4},{4,6},{7,5},{5,7},{10,8},{8,10},{11,... | collective-permute-start | bytes 1179656 | tf_op jit(solution)/shard_map/ppermute | solution.py:34
  103.5 32.4 %collective-permute-start.15 = (bf16[128,1536]{1,0:T(8,128)(2,1)S(1)}, bf16[128,1536]{1,0:T(8,128)(2,1)S(1)}, u32[]{:S(2)}, u32[]{:S(2)}) collective-permute-start(bf16[128,1536]{1,0:T(8,128)(2,1)S(1)} %get-tuple-element.4), channel_id=1, source_target_pairs={{2,0},{0,2},{3,1},{1,3},{6,4},{4,6},{7,5},{5,7},{10,8},{8,10},{11,... | collective-permute-start | bytes 1179656 | tf_op jit(solution)/shard_map/ppermute | solution.py:34
  112.5 24.3 %collective-permute-start.18 = (bf16[256,1536]{1,0:T(8,128)(2,1)S(1)}, bf16[256,1536]{1,0:T(8,128)(2,1)S(1)}, u32[]{:S(2)}, u32[]{:S(2)}) collective-permute-start(bf16[256,1536]{1,0:T(8,128)(2,1)S(1)} %pad_maximum_fusion.7), channel_id=1, source_target_pairs={{1,0},{0,1},{3,2},{2,3},{5,4},{4,5},{7,6},{6,7},{9,8},{8,9},{11,10... | collective-permute-start | bytes 2359304 | tf_op jit(solution)/shard_map/ppermute | solution.py:34
  135.9 3.5 %collective-permute-start.16 = (bf16[256,1536]{1,0:T(8,128)(2,1)S(1)}, bf16[256,1536]{1,0:T(8,128)(2,1)S(1)}, u32[]{:S(2)}, u32[]{:S(2)}) collective-permute-start(bf16[256,1536]{1,0:T(8,128)(2,1)S(1)} %pad_maximum_fusion.6), channel_id=1, source_target_pairs={{1,0},{0,1},{3,2},{2,3},{5,4},{4,5},{7,6},{6,7},{9,8},{8,9},{11,10... | collective-permute-start | bytes 2359304 | tf_op jit(solution)/shard_map/ppermute | solution.py:34
  136.1 8.7 %collective-permute-start.12 = (bf16[256,1536]{1,0:T(8,128)(2,1)S(1)}, bf16[256,1536]{1,0:T(8,128)(2,1)S(1)}, u32[]{:S(2)}, u32[]{:S(2)}) collective-permute-start(bf16[256,1536]{1,0:T(8,128)(2,1)S(1)} %pad_maximum_fusion.4), channel_id=1, source_target_pairs={{1,0},{0,1},{3,2},{2,3},{5,4},{4,5},{7,6},{6,7},{9,8},{8,9},{11,10... | collective-permute-start | bytes 2359304 | tf_op jit(solution)/shard_map/ppermute | solution.py:34
  136.7 5.4 %collective-permute-start.14 = (bf16[256,1536]{1,0:T(8,128)(2,1)S(1)}, bf16[256,1536]{1,0:T(8,128)(2,1)S(1)}, u32[]{:S(2)}, u32[]{:S(2)}) collective-permute-start(bf16[256,1536]{1,0:T(8,128)(2,1)S(1)} %pad_maximum_fusion.5), channel_id=1, source_target_pairs={{1,0},{0,1},{3,2},{2,3},{5,4},{4,5},{7,6},{6,7},{9,8},{8,9},{11,10... | collective-permute-start | bytes 2359304 | tf_op jit(solution)/shard_map/ppermute | solution.py:34

commit v2 on v0

v2 whole, which is shorter than its diff:
```python
import math

import jax
import jax.numpy as jnp
from jax import lax
from jax.experimental import pallas as pl
from jax.experimental.pallas import tpu as pltpu
from jax.sharding import PartitionSpec as P

root_two_pi = 0.7978845608
cubic = 0.044715
f32 = jnp.float32
bf16 = jnp.bfloat16

LANES = 128
WEIGHT_CUTS = (1, 1, 1, 1)
PARTIAL_CUTS = (1, 1, 1, 1)
TILE = 896
VMEM = 48 * 2**20
PARTIAL_COST = 0.01
WEIGHT_COST = 0.1
ANY = pl.BlockSpec(memory_space=pl.ANY)


def gelu_value(value):
    inner = jnp.tanh(root_two_pi * (value + cubic * value * value * value))
    return 0.5 * value * (1.0 + inner)


def gelu_slope(value):
    inner = jnp.tanh(root_two_pi * (value + cubic * value * value * value))
    return 0.5 * (1.0 + inner) + 0.5 * value * (1.0 - inner * inner) * root_two_pi * (
        1.0 + 3.0 * cubic * value * value
    )


def to_next(array, axis, size, hop):
    return lax.ppermute(array, axis, [(i, (i + hop) % size) for i in range(size)])


def from_next(array, axis, size, hop):
    return lax.ppermute(array, axis, [((i + hop) % size, i) for i in range(size)])


def cut(length, shares):
    total, units, done, low, chunks = sum(shares), length // LANES, 0, 0, []
    for share in shares:
        done += share
        high = units * done // total
        if high > low:
            chunks.append((low * LANES, (high - low) * LANES))
        low = high
    return chunks


def tile_of(offset, size, most=TILE):
    step = math.gcd(offset, size)
    best = LANES
    for tile in range(LANES, min(step, most) + 1, LANES):
        if step % tile == 0:
            best = tile
    return best


def call(kernel, name, grid, ins, in_specs, outs, out_specs, after=(), into=None, flops=0):
    extra = list(after) + ([] if into is None else [into])
    count = len(ins)

    def body(*refs):
        kernel(*refs[:count], *refs[count + len(extra) :])

    return pl.pallas_call(
        body,
        grid=grid,
        in_specs=list(in_specs) + [ANY] * len(extra),
        out_specs=list(out_specs),
        out_shape=list(outs),
        input_output_aliases={} if into is None else {count + len(extra) - 1: 0},
        cost_estimate=pl.CostEstimate(
            flops=flops,
            bytes_accessed=1024,
            transcendentals=0,
        ),
        compiler_params=pltpu.CompilerParams(vmem_limit_bytes=VMEM),
        name=name,
    )(*ins, *extra)


def columns(rows, tile, start=0):
    return pl.BlockSpec((rows, tile), lambda i: (0, start + i))


def fixed(shape):
    return pl.BlockSpec(shape, lambda i: (0,) * len(shape))


def split_rows(array, pieces, after):
    rows, width = array.shape[0] // pieces, array.shape[1]

    def kernel(array_ref, *piece_refs):
        for j, ref in enumerate(piece_refs):
            ref[...] = array_ref[j * rows : (j + 1) * rows]

    return call(
        kernel,
        "split_rows",
        (1,),
        [array],
        [fixed(array.shape)],
        [jax.ShapeDtypeStruct((rows, width), array.dtype)] * pieces,
        [fixed((rows, width))] * pieces,
        after,
    )


def hidden_part(preact, offset, size, after):
    block = preact.shape[0]
    tile = tile_of(offset, size)

    def kernel(preact_ref, hidden_ref):
        hidden_ref[...] = gelu_value(preact_ref[...].astype(f32)).astype(bf16)

    return call(
        kernel,
        "hidden_part",
        (size // tile,),
        [preact],
        [columns(block, tile, offset // tile)],
        [jax.ShapeDtypeStruct((block, size), bf16)],
        [columns(block, tile)],
        after,
    )[0]


def slopes(preact, after):
    block, features = preact.shape
    tile = tile_of(0, features)

    def kernel(preact_ref, slope_ref):
        slope_ref[...] = gelu_slope(preact_ref[...].astype(f32))

    return call(
        kernel,
        "slopes",
        (features // tile,),
        [preact],
        [columns(block, tile)],
        [jax.ShapeDtypeStruct((block, features), f32)],
        [columns(block, tile)],
        after,
    )[0]


def tokens_first(grads_ref, others, weight_ref, weights, half):
    dims = (((1,), (1,)), ((), ()))
    product = lax.dot_general(
        grads_ref[:half], weight_ref[...], dims, preferred_element_type=f32
    )
    for other, rows in zip(others, weights):
        product = product + lax.dot_general(
            other[...], rows[...], dims, preferred_element_type=f32
        )
    return product


def partial_products(grads, others, weight, weights, offset, size, block, after):
    half, width = others[0].shape if others else grads.shape
    tile = tile_of(offset, size)
    start = offset // tile
    count = len(others)

    def kernel(grads_ref, weight_ref, *refs):
        own_ref, send_ref = refs[-2:]
        product = tokens_first(grads_ref, refs[:count], weight_ref, refs[count:-2], half)
        own_ref[...] = product[:block]
        send_ref[...] = product[block:].astype(bf16)

    spec = pl.BlockSpec((tile, width), lambda i: (start + i, 0))
    return call(
        kernel,
        "partial_products",
        (size // tile,),
        [grads, weight, *others, *weights],
        [fixed((half, width)), spec] + [fixed((half, width))] * count + [spec] * count,
        [
            jax.ShapeDtypeStruct((block, size), f32),
            jax.ShapeDtypeStruct((half - block, size), bf16),
        ],
        [columns(block, tile), columns(half - block, tile)],
        after,
        flops=int(PARTIAL_COST * 2 * 2 * half * width * size),
    )


def first_products(pieces, other_pieces, place_of, weight, weights, size, block, half, tokens, after):
    tile = tile_of(0, size)
    rows, width = pieces[0][0].shape
    groups = [pieces] + other_pieces
    parts = [part for group in groups for piece in group for part in piece]
    split, entries, count = len(pieces), len(pieces[0]), len(other_pieces)
    held = rows * split

    def kernel(*refs):
        weight_ref, *refs_of = refs[len(parts) : len(parts) + 1 + count]
        outs = refs[len(parts) + 1 + count :]
        grads_ref, other_refs, own_ref, send_ref = outs[0], outs[1:-2], outs[-2], outs[-1]

        @pl.when(pl.program_id(0) == 0)
        def _():
            for j in range(split):
                for s in range(entries):
                    place = place_of(s)
                    at = pl.multiple_of(place * held + j * rows, rows)
                    grads_ref[pl.ds(at, rows)] = refs[j * entries + s][...]

                    @pl.when(place * held < half)
                    def _():
                        for k, other in enumerate(other_refs):
                            source = refs[((k + 1) * split + j) * entries + s]
                            other[pl.ds(at, rows)] = source[...]

        product = tokens_first(grads_ref, other_refs, weight_ref, refs_of, half)
        own_ref[...] = product[:block]
        send_ref[...] = product[block:].astype(bf16)

    spec = pl.BlockSpec((tile, width), lambda i: (i, 0))
    grads, *rest = call(
        kernel,
        "first_products",
        (size // tile,),
        parts + [weight, *weights],
        [fixed((rows, width))] * len(parts) + [spec] * (1 + count),
        [jax.ShapeDtypeStruct((tokens, width), bf16)]
        + [jax.ShapeDtypeStruct((half, width), bf16)] * count
        + [
            jax.ShapeDtypeStruct((block, size), f32),
            jax.ShapeDtypeStruct((half - block, size), bf16),
        ],
        [fixed((tokens, width))]
        + [fixed((half, width))] * count
        + [columns(block, tile), columns(half - block, tile)],
        after,
        flops=int(PARTIAL_COST * 2 * 2 * half * width * size),
    )
    return grads, rest[:-2], rest[-2], rest[-1]


def weight_products(blocks, grads, into, offset, size, scale, after):
    tokens, width = grads.shape
    block, features = blocks[0].shape
    tile = tile_of(offset, size)
    start = offset // tile

    def kernel(*refs):
        grads_ref, out_ref = refs[-2:]
        hidden = jnp.concatenate([ref[...] for ref in refs[:-2]], axis=0)
        product = lax.dot_general(
            hidden, grads_ref[...], (((0,), (0,)), ((), ())), preferred_element_type=f32
        )
        out_ref[...] = (product * scale).astype(bf16)

    return call(
        kernel,
        "weight_products",
        (size // tile,),
        blocks + [grads],
        [columns(block, tile, start)] * len(blocks) + [fixed((tokens, width))],
        [jax.ShapeDtypeStruct((features, width), bf16)],
        [pl.BlockSpec((tile, width), lambda i: (start + i, 0))],
        after,
        into,
        int(WEIGHT_COST * 2 * tokens * width * size),
    )[0]


def last_step(slope, keep, far, into, offset, after):
    block, features = slope.shape
    size = keep.shape[1]
    tile = tile_of(offset, size, size)
    terms = list(far)

    def kernel(slope_ref, keep_ref, *refs):
        total = keep_ref[...]
        for ref in refs[:-1]:
            total = total + ref[...].astype(f32)
        refs[-1][...] = (total * slope_ref[...]).astype(bf16)

    return call(
        kernel,
        "last_step",
        (size // tile,),
        [slope, keep] + terms,
        [columns(block, tile, offset // tile)] + [columns(block, tile)] * (1 + len(terms)),
        [jax.ShapeDtypeStruct((block, features), bf16)],
        [columns(block, tile, offset // tile)],
        after,
        into,
    )[0]


def solution(mesh):
    rows, cols, depths = mesh.shape["row"], mesh.shape["col"], mesh.shape["depth"]

    def per_device(preact, weight, out_grad):
        block, features = preact.shape
        row_tokens, width = out_grad.shape
        tokens = row_tokens * rows
        scale = 1.0 / math.sqrt(tokens)
        half = cols * block
        per_block = block // row_tokens
        ring = rows <= 4

        hidden = [hidden_part(preact, 0, features, [])]
        parts = split_rows(out_grad, 2 if ring else 1, [hidden[0]])
        hidden += [from_next(hidden[0], "col", cols, dx) for dx in range(1, cols)]
        slope = slopes(preact, [hidden[0]])

        if ring:
            pieces = [[part] for part in parts]
            for hop in range(rows - 1):
                for piece in pieces:
                    piece.append(to_next(piece[-1], "row", rows, 1))
                if hop == 0:
                    pieces[-1][-1], slope = lax.optimization_barrier((pieces[-1][-1], slope))
        else:
            whole = lax.all_gather(parts[0], "row", axis=0, tiled=False)
            z = lax.axis_index("row")
            pieces = [
                [
                    lax.dynamic_index_in_dim(whole, lax.rem(z - s + rows, rows), 0, False)
                    for s in range(rows)
                ]
            ]

        def place_of(s):
            row = lax.rem(lax.axis_index("row") - s + rows, rows)
            owner = row // per_block
            dx = lax.rem(owner // depths - lax.axis_index("col") + cols, cols)
            dd = lax.rem(lax.rem(owner, depths) - lax.axis_index("depth") + depths, depths)
            return (dd * cols + dx) * per_block + lax.rem(row, per_block)

        hops = range(1, depths)
        weights = [from_next(weight, "depth", depths, dd) for dd in hops]
        if ring:
            for piece in pieces:
                *piece[:-1], _ = lax.optimization_barrier((*piece[:-1], pieces[-1][-2]))
        other_pieces = [
            [[from_next(part, "depth", depths, dd) for part in piece] for piece in pieces]
            for dd in hops
        ]

        chunks = cut(features, PARTIAL_CUTS)
        count = len(chunks)
        owns, far = [], []
        for c, (offset, size) in enumerate(chunks):
            if c == 0:
                grads, others, own, send = first_products(
                    pieces, other_pieces, place_of, weight, weights, size, block, half, tokens,
                    [slope],
                )
            else:
                own, send = partial_products(
                    grads, others, weight, weights, offset, size, block, owns[-1:]
                )
            owns.append(own)
            far.append(
                [
                    to_next(send[(dx - 1) * block : dx * block], "col", cols, dx)
                    for dx in range(1, cols)
                ]
            )

        *blocks, _ = lax.optimization_barrier((*hidden, owns[min(1, count - 1)]))
        blocks += [from_next(part, "depth", depths, dd) for dd in hops for part in blocks]
        weight_grad = None
        for k, (offset, size) in enumerate(cut(features, WEIGHT_CUTS)):
            after = owns[-1:] if k == 0 else far[k - 1][-1:] if k < count else []
            weight_grad = weight_products(blocks, grads, weight_grad, offset, size, scale, after)
        preact_grad = None
        for c in range(count):
            preact_grad = last_step(
                slope, owns[c], far[c], preact_grad, chunks[c][0], [weight_grad] if c == 0 else []
            )
        return preact_grad, weight_grad

    return jax.shard_map(
        per_device,
        mesh=mesh,
        in_specs=(
            P(("group", "col", "depth"), "row"),
            P("row", ("col", "depth")),
            P(("group", "row"), ("col", "depth")),
        ),
        out_specs=(P(("group", "col", "depth"), "row"), P(("group", "row"), ("col", "depth"))),
        check_vma=False,
    )
```

time: 589 us -> 100 us (0.17)
  waiting for transfers between devices: 480 us -> 26.6 us
  matrix products: 57.3 us -> 0 us
  Pallas kernels: 0 us -> 54.1 us
  blocking collectives: 36.4 us -> 0 us
  starting transfers between devices: 0.11 us -> 14.3 us
  between operations: 13.7 us -> 0.73 us
    all_gather x3 -> x0, waiting for transfers between devices: 478 us -> none  [the longest x1 416 us: per_device(): lax.all_gather(weight, ('col', 'depth'), axis=1, tiled=True)]
    dot_general x2 -> x0, matrix products: 57.3 us -> none  [the longest x1 32.7 us: per_device(): lax.dot_general(own_grad, lax.all_gather(weight, ('col', 'depth'), axis=1...]
    pallas_call x0 -> x15, Pallas kernels: none -> 54.1 us  [call(): pl.pallas_call(body, grid=grid, in_specs=list(in_specs) + [ANY] * len(ext...]
    all_to_all x1 -> x0, blocking collectives: 36.4 us -> none  [per_device(): lax.all_to_all(all_grad, ('col', 'depth'), split_axis=0, concat_axis=1, t...]
    ppermute x0 -> x22, waiting for transfers between devices: none -> 26.6 us  [the longest x10 23.9 us: to_next(): lax.ppermute(array, axis, [(i, (i + hop) % size) for i in range(size)])]
    ppermute x0 -> x22, starting transfers between devices: none -> 14.3 us  [the longest x10 9.04 us: to_next(): lax.ppermute(array, axis, [(i, (i + hop) % size) for i in range(size)])]
  transfers between devices with their start and end apart: 3 -> 22, of which waited for: 3 -> 8; matrix products, arithmetic and copies ran while one was open for 4% -> 0% of each run, Pallas kernels for 0% -> 53%
where the time goes in v2:
time: 100 us; the launch traced here: 99.7 us
  Pallas kernels  54.1 us (54%)
  waiting for transfers between devices  26.6 us (27%)
  starting transfers between devices  14.3 us (14%)
  local copies, waits for them, and re-layouts  4.01 us (4%)
    pallas_call x15, Pallas kernels, call(): pl.pallas_call(body, grid=grid, in_specs=list(in_specs) + [ANY] * len(ext...  54.1 us
    ppermute x10, waiting for transfers between devices, to_next(): lax.ppermute(array, axis, [(i, (i + hop) % size) for i in range(size)])  23.9 us
    ppermute x10, starting transfers between devices, to_next(): lax.ppermute(array, axis, [(i, (i + hop) % size) for i in range(size)])  9.04 us
    ppermute x12, starting transfers between devices, from_next(): lax.ppermute(array, axis, [((i + hop) % size, i) for i in range(size)])  5.22 us
    unnamed x10, local copies, waits for them, and re-layouts  4.01 us
    ppermute x12, waiting for transfers between devices, from_next(): lax.ppermute(array, axis, [((i + hop) % size, i) for i in range(size)])  2.63 us
  transfers between devices with their start and end apart: 22, of which 8 were waited for; matrix products, arithmetic and copies ran while one was open for 0% of the time, Pallas kernels for 53%

profile of v2, /device:TPU:0, one launch (start us, length us, event | category | flops | bytes accessed | tf_op | source)
XLA Modules:
  0.0 99.7 jit_solution(11803886708103380292)
XLA Ops:
  0.6 0.5 collective-permute-start.14
  1.1 1.4 %copy-done.2 = bf16[128,6144]{1,0:T(8,128)(2,1)S(1)} copy-done((bf16[128,6144]{1,0:T(8,128)(2,1)S(1)}, bf16[128,6144]{1,0:T(8,128)(2,1)}, u32[]{:S(2)}) %copy-start.2) | copy-done | bytes 1572888
  2.6 1.4 %hidden_part.1.refs_1_.refs_0_ = bf16[128,6144]{1,0:T(8,128)(2,1)S(1)} custom-call(bf16[128,6144]{1,0:T(8,128)(2,1)S(1)} %copy-done.2), custom_call_target="tpu_custom_call" | custom-call | bytes 1024 | tf_op jit(solution)/shard_map/hidden_part/pallas_call | solution.py:72
  4.0 2.6 %collective-permute-start.19 = (bf16[128,6144]{1,0:T(8,128)(2,1)S(1)}, bf16[128,6144]{1,0:T(8,128)(2,1)S(1)}, u32[]{:S(2)}, u32[]{:S(2)}) collective-permute-start(bf16[128,6144]{1,0:T(8,128)(2,1)S(1)} %hidden_part.1.refs_1_.refs_0_), channel_id=1, source_target_pairs={{2,0},{0,2},{3,1},{1,3},{6,4},{4,6},{7,5},{5,7},{10,8},{8,10},{11,... | collective-permute-start | bytes 4718600 | tf_op jit(solution)/shard_map/ppermute | solution.py:42
  6.5 0.0 copy-done.3
  6.6 1.6 %collective-permute-start.1 = (bf16[64,1536]{1,0:T(8,128)(2,1)S(1)}, bf16[64,1536]{1,0:T(8,128)(2,1)S(1)}, u32[]{:S(2)}, u32[]{:S(2)}) collective-permute-start(bf16[64,1536]{1,0:T(8,128)(2,1)S(1)} %get-tuple-element.28.refs_0_), channel_id=1, source_target_pairs={{0,4},{4,8},{8,12},{12,0},{1,5},{5,9},{9,13},{13,1},{2,6},{6,10},{... | collective-permute-start | bytes 589832 | tf_op jit(solution)/shard_map/ppermute | solution.py:38
  8.2 1.6 %collective-permute-start = (bf16[64,1536]{1,0:T(8,128)(2,1)S(1)}, bf16[64,1536]{1,0:T(8,128)(2,1)S(1)}, u32[]{:S(2)}, u32[]{:S(2)}) collective-permute-start(bf16[64,1536]{1,0:T(8,128)(2,1)S(1)} %get-tuple-element.31.refs_4_), channel_id=1, source_target_pairs={{0,4},{4,8},{8,12},{12,0},{1,5},{5,9},{9,13},{13,1},{2,6},{6,10},{... | collective-permute-start | bytes 589832 | tf_op jit(solution)/shard_map/ppermute | solution.py:38
  9.8 6.4 %collective-permute-done.1.refs_1_ = bf16[64,1536]{1,0:T(8,128)(2,1)S(1)} collective-permute-done((bf16[64,1536]{1,0:T(8,128)(2,1)S(1)}, bf16[64,1536]{1,0:T(8,128)(2,1)S(1)}, u32[]{:S(2)}, u32[]{:S(2)}) %collective-permute-start.1) | collective-permute-done | bytes 196640 | tf_op jit(solution)/shard_map/ppermute | solution.py:38
  16.2 0.0 collective-permute-start.2
  16.2 4.4 %slopes.1.refs_18_.refs_0_ = f32[128,6144]{1,0:T(8,128)} custom-call(bf16[128,6144]{1,0:T(8,128)(2,1)S(1)} %copy-done.2, bf16[128,6144]{1,0:T(8,128)(2,1)S(1)} %hidden_part.1.refs_1_.refs_0_), custom_call_target="tpu_custom_call" | custom-call | bytes 1024 | tf_op jit(solution)/shard_map/slopes/pallas_call | solution.py:72
  20.6 0.0 collective-permute-done.refs_5_
  20.6 1.4 %collective-permute-start.3 = (bf16[64,1536]{1,0:T(8,128)(2,1)S(1)}, bf16[64,1536]{1,0:T(8,128)(2,1)S(1)}, u32[]{:S(2)}, u32[]{:S(2)}) collective-permute-start(bf16[64,1536]{1,0:T(8,128)(2,1)S(1)} %collective-permute-done.refs_5_), channel_id=1, source_target_pairs={{0,4},{4,8},{8,12},{12,0},{1,5},{5,9},{9,13},{13,1},{2,6},{6,10},{... | collective-permute-start | bytes 589832 | tf_op jit(solution)/shard_map/ppermute | solution.py:38
  22.0 2.0 %collective-permute-done.2.refs_2_ = bf16[64,1536]{1,0:T(8,128)(2,1)S(1)} collective-permute-done((bf16[64,1536]{1,0:T(8,128)(2,1)S(1)}, bf16[64,1536]{1,0:T(8,128)(2,1)S(1)}, u32[]{:S(2)}, u32[]{:S(2)}) %collective-permute-start.2) | collective-permute-done | bytes 196640 | tf_op jit(solution)/shard_map/ppermute | solution.py:38
  24.0 0.3 collective-permute-start.4
  24.3 5.5 %collective-permute-done.3.refs_6_ = bf16[64,1536]{1,0:T(8,128)(2,1)S(1)} collective-permute-done((bf16[64,1536]{1,0:T(8,128)(2,1)S(1)}, bf16[64,1536]{1,0:T(8,128)(2,1)S(1)}, u32[]{:S(2)}, u32[]{:S(2)}) %collective-permute-start.3) | collective-permute-done | bytes 196640 | tf_op jit(solution)/shard_map/ppermute | solution.py:38
  29.8 0.0 collective-permute-start.6
  29.8 0.5 collective-permute-start.7
  30.3 2.1 %collective-permute-done.4.refs_3_ = bf16[64,1536]{1,0:T(8,128)(2,1)S(1)} collective-permute-done((bf16[64,1536]{1,0:T(8,128)(2,1)S(1)}, bf16[64,1536]{1,0:T(8,128)(2,1)S(1)}, u32[]{:S(2)}, u32[]{:S(2)}) %collective-permute-start.4) | collective-permute-done | bytes 196640 | tf_op jit(solution)/shard_map/ppermute | solution.py:38
  32.4 0.0 collective-permute-start.8
  32.4 0.0 collective-permute-done.6.refs_8_
  32.4 0.5 collective-permute-start.10
  32.9 0.0 collective-permute-done.7.refs_9_
  32.9 0.1 collective-permute-start.11
  33.0 0.9 collective-permute-done.8.refs_10_
  33.8 0.0 collective-permute-start.5
  33.8 0.3 collective-permute-done.10.refs_12_
  34.1 0.2 collective-permute-start.12
  34.3 0.0 collective-permute-done.11.refs_13_
  34.4 0.2 collective-permute-start.9
  34.6 7.9 %collective-permute-done.5.refs_7_ = bf16[64,1536]{1,0:T(8,128)(2,1)S(1)} collective-permute-done((bf16[64,1536]{1,0:T(8,128)(2,1)S(1)}, bf16[64,1536]{1,0:T(8,128)(2,1)S(1)}, u32[]{:S(2)}, u32[]{:S(2)}) %collective-permute-start.5) | collective-permute-done | bytes 196640 | tf_op jit(solution)/shard_map/ppermute | solution.py:38
  42.6 0.0 collective-permute-start.13
  42.6 0.0 collective-permute-done.12.refs_14_
  42.6 0.0 collective-permute-done.9.refs_11_
  42.6 1.4 %collective-permute-done.13.refs_15_ = bf16[64,1536]{1,0:T(8,128)(2,1)S(1)} collective-permute-done((bf16[64,1536]{1,0:T(8,128)(2,1)S(1)}, bf16[64,1536]{1,0:T(8,128)(2,1)S(1)}, u32[]{:S(2)}, u32[]{:S(2)}) %collective-permute-start.13) | collective-permute-done | bytes 196640 | tf_op jit(solution)/shard_map/ppermute | solution.py:42
  44.0 0.0 collective-permute-done.14.refs_17_.refs_3_
  44.0 5.5 %first_products.1 = (bf16[512,1536]{1,0:T(8,128)(2,1)}, bf16[256,1536]{1,0:T(8,128)(2,1)S(1)}, f32[128,1536]{1,0:T(8,128)S(1)}, bf16[128,1536]{1,0:T(8,128)(2,1)S(1)}) custom-call(bf16[64,1536]{1,0:T(8,128)(2,1)S(1)} %get-tuple-element.28.refs_0_, bf16[64,1536]{1,0:T(8,128)(2,1)S(1)} %collective-permute-done.1.refs_1_, ...), custom_call_target="tpu_custom_call" | custom-call | flops 24159192 | bytes 1024 | tf_op jit(solution)/shard_map/first_products/pallas_call | solution.py:72
  49.6 0.0 copy-start.1
  49.6 1.4 %copy-done.1 = bf16[512,1536]{1,0:T(8,128)(2,1)S(1)} copy-done((bf16[512,1536]{1,0:T(8,128)(2,1)S(1)}, bf16[512,1536]{1,0:T(8,128)(2,1)}, u32[]{:S(2)}) %copy-start.1) | copy-done | bytes 1572888
  51.0 5.3 %partial_products.3 = (f32[128,1536]{1,0:T(8,128)S(1)}, bf16[128,1536]{1,0:T(8,128)(2,1)S(1)}) custom-call(bf16[512,1536]{1,0:T(8,128)(2,1)S(1)} %copy-done.1, bf16[6144,1536]{1,0:T(8,128)(2,1)} %refs_1_.5, bf16[256,1536]{1,0:T(8,128)(2,1)S(1)} %get-tuple-element.35.refs_2_, bf16[6144,1536]{1,0:T(8,128)(2,1)} %collective-permute-done.14.refs_17_.refs_3_, ...), custom_call_target="tpu_custom_call" | custom-call | flops 24159192 | bytes 1024 | tf_op jit(solution)/shard_map/partial_products/pallas_call | solution.py:72
  56.3 0.0 collective-permute-done.19.refs_1_
  56.3 0.2 collective-permute-start.20
  56.5 0.4 collective-permute-start.21
  56.9 0.7 collective-permute-start.18
  57.5 1.4 %collective-permute-start.17 = (bf16[128,1536]{1,0:T(8,128)(2,1)S(1)}, bf16[128,1536]{1,0:T(8,128)(2,1)S(1)}, u32[]{:S(2)}, u32[]{:S(2)}) collective-permute-start(bf16[128,1536]{1,0:T(8,128)(2,1)S(1)} %get-tuple-element.42), channel_id=1, source_target_pairs={{0,2},{2,0},{1,3},{3,1},{4,6},{6,4},{5,7},{7,5},{8,10},{10,8},{9,1... | collective-permute-start | bytes 1179656 | tf_op jit(solution)/shard_map/ppermute | solution.py:38
  58.9 5.3 %partial_products.4 = (f32[128,1536]{1,0:T(8,128)S(1)}, bf16[128,1536]{1,0:T(8,128)(2,1)S(1)}) custom-call(bf16[512,1536]{1,0:T(8,128)(2,1)S(1)} %copy-done.1, bf16[6144,1536]{1,0:T(8,128)(2,1)} %refs_1_.5, bf16[256,1536]{1,0:T(8,128)(2,1)S(1)} %get-tuple-element.35.refs_2_, bf16[6144,1536]{1,0:T(8,128)(2,1)} %collective-permute-done.14.refs_17_.refs_3_, ...), custom_call_target="tpu_custom_call" | custom-call | flops 24159192 | bytes 1024 | tf_op jit(solution)/shard_map/partial_products/pallas_call | solution.py:72
  64.2 0.7 collective-permute-start.16
  64.9 5.3 %partial_products.5 = (f32[128,1536]{1,0:T(8,128)S(1)}, bf16[128,1536]{1,0:T(8,128)(2,1)S(1)}) custom-call(bf16[512,1536]{1,0:T(8,128)(2,1)S(1)} %copy-done.1, bf16[6144,1536]{1,0:T(8,128)(2,1)} %refs_1_.5, bf16[256,1536]{1,0:T(8,128)(2,1)S(1)} %get-tuple-element.35.refs_2_, bf16[6144,1536]{1,0:T(8,128)(2,1)} %collective-permute-done.14.refs_17_.refs_3_, ...), custom_call_target="tpu_custom_call" | custom-call | flops 24159192 | bytes 1024 | tf_op jit(solution)/shard_map/partial_products/pallas_call | solution.py:72
  70.2 0.0 collective-permute-done.20.refs_2_
  70.2 1.4 %collective-permute-start.15 = (bf16[128,1536]{1,0:T(8,128)(2,1)S(1)}, bf16[128,1536]{1,0:T(8,128)(2,1)S(1)}, u32[]{:S(2)}, u32[]{:S(2)}) collective-permute-start(bf16[128,1536]{1,0:T(8,128)(2,1)S(1)} %get-tuple-element.40), channel_id=1, source_target_pairs={{0,2},{2,0},{1,3},{3,1},{4,6},{6,4},{5,7},{7,5},{8,10},{10,8},{9,1... | collective-permute-start | bytes 1179656 | tf_op jit(solution)/shard_map/ppermute | solution.py:38
  71.7 0.0 collective-permute-done.21.refs_3_
  71.7 1.2 %copy-done.4 = bf16[128,6144]{1,0:T(8,128)(2,1)} copy-done((bf16[128,6144]{1,0:T(8,128)(2,1)}, bf16[128,6144]{1,0:T(8,128)(2,1)S(1)}, u32[]{:S(2)}) %copy-start.4) | copy-done | bytes 1572888
  72.9 5.8 %weight_products.4.refs_6_ = bf16[6144,1536]{1,0:T(8,128)(2,1)} custom-call(bf16[128,6144]{1,0:T(8,128)(2,1)S(1)} %hidden_part.1.refs_1_.refs_0_, bf16[128,6144]{1,0:T(8,128)(2,1)S(1)} %collective-permute-done.19.refs_1_, bf16[128,6144]{1,0:T(8,128)(2,1)S(1)} %collective-permute-done.20.refs_2_, bf16[128,6144]{1,0:T(8,128)(2,1)} %copy-done.4, ...), custom_call_target="tpu_custom_call" | custom-call | flops 241591904 | bytes 1024 | tf_op jit(solution)/shard_map/weight_products/pallas_call | solution.py:72
  78.7 0.0 collective-permute-done.18.refs_5_.refs_2_
  78.7 5.8 %weight_products.5.refs_6_ = bf16[6144,1536]{1,0:T(8,128)(2,1)} custom-call(bf16[128,6144]{1,0:T(8,128)(2,1)S(1)} %hidden_part.1.refs_1_.refs_0_, bf16[128,6144]{1,0:T(8,128)(2,1)S(1)} %collective-permute-done.19.refs_1_, bf16[128,6144]{1,0:T(8,128)(2,1)S(1)} %collective-permute-done.20.refs_2_, ...), custom_call_target="tpu_custom_call", output_to_operand_aliasing={{}: (6, {})} | custom-call | flops 241591904 | bytes 1024 | tf_op jit(solution)/shard_map/weight_products/pallas_call | solution.py:72
  84.5 0.0 collective-permute-done.17.refs_5_.refs_2_
  84.5 5.8 %weight_products.6.refs_6_ = bf16[6144,1536]{1,0:T(8,128)(2,1)} custom-call(bf16[128,6144]{1,0:T(8,128)(2,1)S(1)} %hidden_part.1.refs_1_.refs_0_, bf16[128,6144]{1,0:T(8,128)(2,1)S(1)} %collective-permute-done.19.refs_1_, bf16[128,6144]{1,0:T(8,128)(2,1)S(1)} %collective-permute-done.20.refs_2_, ...), custom_call_target="tpu_custom_call", output_to_operand_aliasing={{}: (6, {})} | custom-call | flops 241591904 | bytes 1024 | tf_op jit(solution)/shard_map/weight_products/pallas_call | solution.py:72
  90.4 0.0 collective-permute-done.16.refs_5_.refs_2_
  90.4 6.0 %weight_products.7.refs_3_ = bf16[6144,1536]{1,0:T(8,128)(2,1)} custom-call(bf16[128,6144]{1,0:T(8,128)(2,1)S(1)} %hidden_part.1.refs_1_.refs_0_, bf16[128,6144]{1,0:T(8,128)(2,1)S(1)} %collective-permute-done.19.refs_1_, bf16[128,6144]{1,0:T(8,128)(2,1)S(1)} %collective-permute-done.20.refs_2_, ...), custom_call_target="tpu_custom_call", output_to_operand_aliasing={{}: (6, {})} | custom-call | flops 241591904 | bytes 1024 | tf_op jit(solution)/shard_map/weight_products/pallas_call | solution.py:72
  96.3 0.0 copy-done
  96.3 0.8 last_step.4.refs_3_
  97.2 0.8 last_step.5.refs_3_
  98.0 0.8 last_step.6.refs_3_
  98.9 0.0 collective-permute-done.15.refs_2_
  98.9 0.8 last_step.7
  (5 shorter events, 0.0 us)
Async XLA Ops:
  0.6 43.4 %collective-permute-start.14 = (bf16[6144,1536]{1,0:T(8,128)(2,1)}, bf16[6144,1536]{1,0:T(8,128)(2,1)}, u32[]{:S(2)}, u32[]{:S(2)}) collective-permute-start(bf16[6144,1536]{1,0:T(8,128)(2,1)} %refs_1_.5), channel_id=1, source_target_pairs={{1,0},{0,1},{3,2},{2,3},{5,4},{4,5},{7,6},{6,7},{9,8},{8,9},{11,10... | collective-permute-start | bytes 56623112 | tf_op jit(solution)/shard_map/ppermute | solution.py:42
  1.1 1.4 %copy-start.2 = (bf16[128,6144]{1,0:T(8,128)(2,1)S(1)}, bf16[128,6144]{1,0:T(8,128)(2,1)}, u32[]{:S(2)}) copy-start(bf16[128,6144]{1,0:T(8,128)(2,1)} %refs_0_.5) | copy-start | bytes 4718596
  2.6 4.0 %copy-start.3 = (bf16[128,1536]{1,0:T(8,128)(2,1)S(1)}, bf16[128,1536]{1,0:T(8,128)(2,1)}, u32[]{:S(2)}) copy-start(bf16[128,1536]{1,0:T(8,128)(2,1)} %refs_0_.4) | copy-start | bytes 1179652
  4.0 52.3 %collective-permute-start.19 = (bf16[128,6144]{1,0:T(8,128)(2,1)S(1)}, bf16[128,6144]{1,0:T(8,128)(2,1)S(1)}, u32[]{:S(2)}, u32[]{:S(2)}) collective-permute-start(bf16[128,6144]{1,0:T(8,128)(2,1)S(1)} %hidden_part.1.refs_1_.refs_0_), channel_id=1, source_target_pairs={{2,0},{0,2},{3,1},{1,3},{6,4},{4,6},{7,5},{5,7},{10,8},{8,10},{11,... | collective-permute-start | bytes 4718600 | tf_op jit(solution)/shard_map/ppermute | solution.py:42
  6.6 9.6 %collective-permute-start.1 = (bf16[64,1536]{1,0:T(8,128)(2,1)S(1)}, bf16[64,1536]{1,0:T(8,128)(2,1)S(1)}, u32[]{:S(2)}, u32[]{:S(2)}) collective-permute-start(bf16[64,1536]{1,0:T(8,128)(2,1)S(1)} %get-tuple-element.28.refs_0_), channel_id=1, source_target_pairs={{0,4},{4,8},{8,12},{12,0},{1,5},{5,9},{9,13},{13,1},{2,6},{6,10},{... | collective-permute-start | bytes 589832 | tf_op jit(solution)/shard_map/ppermute | solution.py:38
  8.2 12.4 %collective-permute-start = (bf16[64,1536]{1,0:T(8,128)(2,1)S(1)}, bf16[64,1536]{1,0:T(8,128)(2,1)S(1)}, u32[]{:S(2)}, u32[]{:S(2)}) collective-permute-start(bf16[64,1536]{1,0:T(8,128)(2,1)S(1)} %get-tuple-element.31.refs_4_), channel_id=1, source_target_pairs={{0,4},{4,8},{8,12},{12,0},{1,5},{5,9},{9,13},{13,1},{2,6},{6,10},{... | collective-permute-start | bytes 589832 | tf_op jit(solution)/shard_map/ppermute | solution.py:38
  16.2 7.8 %collective-permute-start.2 = (bf16[64,1536]{1,0:T(8,128)(2,1)S(1)}, bf16[64,1536]{1,0:T(8,128)(2,1)S(1)}, u32[]{:S(2)}, u32[]{:S(2)}) collective-permute-start(bf16[64,1536]{1,0:T(8,128)(2,1)S(1)} %collective-permute-done.1.refs_1_), channel_id=1, source_target_pairs={{0,4},{4,8},{8,12},{12,0},{1,5},{5,9},{9,13},{13,1},{2,6},{6,10},{... | collective-permute-start | bytes 589832 | tf_op jit(solution)/shard_map/ppermute | solution.py:38
  20.6 9.2 %collective-permute-start.3 = (bf16[64,1536]{1,0:T(8,128)(2,1)S(1)}, bf16[64,1536]{1,0:T(8,128)(2,1)S(1)}, u32[]{:S(2)}, u32[]{:S(2)}) collective-permute-start(bf16[64,1536]{1,0:T(8,128)(2,1)S(1)} %collective-permute-done.refs_5_), channel_id=1, source_target_pairs={{0,4},{4,8},{8,12},{12,0},{1,5},{5,9},{9,13},{13,1},{2,6},{6,10},{... | collective-permute-start | bytes 589832 | tf_op jit(solution)/shard_map/ppermute | solution.py:38
  24.0 8.4 %collective-permute-start.4 = (bf16[64,1536]{1,0:T(8,128)(2,1)S(1)}, bf16[64,1536]{1,0:T(8,128)(2,1)S(1)}, u32[]{:S(2)}, u32[]{:S(2)}) collective-permute-start(bf16[64,1536]{1,0:T(8,128)(2,1)S(1)} %collective-permute-done.2.refs_2_), channel_id=1, source_target_pairs={{0,4},{4,8},{8,12},{12,0},{1,5},{5,9},{9,13},{13,1},{2,6},{6,10},{... | collective-permute-start | bytes 589832 | tf_op jit(solution)/shard_map/ppermute | solution.py:38
  29.8 2.6 %collective-permute-start.6 = (bf16[64,1536]{1,0:T(8,128)(2,1)S(1)}, bf16[64,1536]{1,0:T(8,128)(2,1)S(1)}, u32[]{:S(2)}, u32[]{:S(2)}) collective-permute-start(bf16[64,1536]{1,0:T(8,128)(2,1)S(1)} %get-tuple-element.28.refs_0_), channel_id=1, source_target_pairs={{1,0},{0,1},{3,2},{2,3},{5,4},{4,5},{7,6},{6,7},{9,8},{8,9},{11,10... | collective-permute-start | bytes 589832 | tf_op jit(solution)/shard_map/ppermute | solution.py:42
  29.8 3.1 %collective-permute-start.7 = (bf16[64,1536]{1,0:T(8,128)(2,1)S(1)}, bf16[64,1536]{1,0:T(8,128)(2,1)S(1)}, u32[]{:S(2)}, u32[]{:S(2)}) collective-permute-start(bf16[64,1536]{1,0:T(8,128)(2,1)S(1)} %collective-permute-done.1.refs_1_), channel_id=1, source_target_pairs={{1,0},{0,1},{3,2},{2,3},{5,4},{4,5},{7,6},{6,7},{9,8},{8,9},{11,10... | collective-permute-start | bytes 589832 | tf_op jit(solution)/shard_map/ppermute | solution.py:42
  32.4 1.4 %collective-permute-start.8 = (bf16[64,1536]{1,0:T(8,128)(2,1)S(1)}, bf16[64,1536]{1,0:T(8,128)(2,1)S(1)}, u32[]{:S(2)}, u32[]{:S(2)}) collective-permute-start(bf16[64,1536]{1,0:T(8,128)(2,1)S(1)} %collective-permute-done.2.refs_2_), channel_id=1, source_target_pairs={{1,0},{0,1},{3,2},{2,3},{5,4},{4,5},{7,6},{6,7},{9,8},{8,9},{11,10... | collective-permute-start | bytes 589832 | tf_op jit(solution)/shard_map/ppermute | solution.py:42
  32.4 1.7 %collective-permute-start.10 = (bf16[64,1536]{1,0:T(8,128)(2,1)S(1)}, bf16[64,1536]{1,0:T(8,128)(2,1)S(1)}, u32[]{:S(2)}, u32[]{:S(2)}) collective-permute-start(bf16[64,1536]{1,0:T(8,128)(2,1)S(1)} %get-tuple-element.31.refs_4_), channel_id=1, source_target_pairs={{1,0},{0,1},{3,2},{2,3},{5,4},{4,5},{7,6},{6,7},{9,8},{8,9},{11,10... | collective-permute-start | bytes 589832 | tf_op jit(solution)/shard_map/ppermute | solution.py:42
  32.9 1.5 %collective-permute-start.11 = (bf16[64,1536]{1,0:T(8,128)(2,1)S(1)}, bf16[64,1536]{1,0:T(8,128)(2,1)S(1)}, u32[]{:S(2)}, u32[]{:S(2)}) collective-permute-start(bf16[64,1536]{1,0:T(8,128)(2,1)S(1)} %collective-permute-done.refs_5_), channel_id=1, source_target_pairs={{1,0},{0,1},{3,2},{2,3},{5,4},{4,5},{7,6},{6,7},{9,8},{8,9},{11,10... | collective-permute-start | bytes 589832 | tf_op jit(solution)/shard_map/ppermute | solution.py:42
  33.8 8.7 %collective-permute-start.5 = (bf16[64,1536]{1,0:T(8,128)(2,1)S(1)}, bf16[64,1536]{1,0:T(8,128)(2,1)S(1)}, u32[]{:S(2)}, u32[]{:S(2)}) collective-permute-start(bf16[64,1536]{1,0:T(8,128)(2,1)S(1)} %collective-permute-done.3.refs_6_), channel_id=1, source_target_pairs={{0,4},{4,8},{8,12},{12,0},{1,5},{5,9},{9,13},{13,1},{2,6},{6,10},{... | collective-permute-start | bytes 589832 | tf_op jit(solution)/shard_map/ppermute | solution.py:38
  34.1 8.5 %collective-permute-start.12 = (bf16[64,1536]{1,0:T(8,128)(2,1)S(1)}, bf16[64,1536]{1,0:T(8,128)(2,1)S(1)}, u32[]{:S(2)}, u32[]{:S(2)}) collective-permute-start(bf16[64,1536]{1,0:T(8,128)(2,1)S(1)} %collective-permute-done.3.refs_6_), channel_id=1, source_target_pairs={{1,0},{0,1},{3,2},{2,3},{5,4},{4,5},{7,6},{6,7},{9,8},{8,9},{11,10... | collective-permute-start | bytes 589832 | tf_op jit(solution)/shard_map/ppermute | solution.py:42
  34.4 8.2 %collective-permute-start.9 = (bf16[64,1536]{1,0:T(8,128)(2,1)S(1)}, bf16[64,1536]{1,0:T(8,128)(2,1)S(1)}, u32[]{:S(2)}, u32[]{:S(2)}) collective-permute-start(bf16[64,1536]{1,0:T(8,128)(2,1)S(1)} %collective-permute-done.4.refs_3_), channel_id=1, source_target_pairs={{1,0},{0,1},{3,2},{2,3},{5,4},{4,5},{7,6},{6,7},{9,8},{8,9},{11,10... | collective-permute-start | bytes 589832 | tf_op jit(solution)/shard_map/ppermute | solution.py:42
  42.6 1.4 %collective-permute-start.13 = (bf16[64,1536]{1,0:T(8,128)(2,1)S(1)}, bf16[64,1536]{1,0:T(8,128)(2,1)S(1)}, u32[]{:S(2)}, u32[]{:S(2)}) collective-permute-start(bf16[64,1536]{1,0:T(8,128)(2,1)S(1)} %collective-permute-done.5.refs_7_), channel_id=1, source_target_pairs={{1,0},{0,1},{3,2},{2,3},{5,4},{4,5},{7,6},{6,7},{9,8},{8,9},{11,10... | collective-permute-start | bytes 589832 | tf_op jit(solution)/shard_map/ppermute | solution.py:42
  49.6 1.4 %copy-start.1 = (bf16[512,1536]{1,0:T(8,128)(2,1)S(1)}, bf16[512,1536]{1,0:T(8,128)(2,1)}, u32[]{:S(2)}) copy-start(bf16[512,1536]{1,0:T(8,128)(2,1)} %get-tuple-element.34.refs_0_.refs_4_) | copy-start | bytes 4718596
  56.3 13.9 %collective-permute-start.20 = (bf16[128,6144]{1,0:T(8,128)(2,1)S(1)}, bf16[128,6144]{1,0:T(8,128)(2,1)S(1)}, u32[]{:S(2)}, u32[]{:S(2)}) collective-permute-start(bf16[128,6144]{1,0:T(8,128)(2,1)S(1)} %hidden_part.1.refs_1_.refs_0_), channel_id=1, source_target_pairs={{1,0},{0,1},{3,2},{2,3},{5,4},{4,5},{7,6},{6,7},{9,8},{8,9},{11,10... | collective-permute-start | bytes 4718600 | tf_op jit(solution)/shard_map/ppermute | solution.py:42
  56.5 15.2 %collective-permute-start.21 = (bf16[128,6144]{1,0:T(8,128)(2,1)S(1)}, bf16[128,6144]{1,0:T(8,128)(2,1)S(1)}, u32[]{:S(2)}, u32[]{:S(2)}) collective-permute-start(bf16[128,6144]{1,0:T(8,128)(2,1)S(1)} %collective-permute-done.19.refs_1_), channel_id=1, source_target_pairs={{1,0},{0,1},{3,2},{2,3},{5,4},{4,5},{7,6},{6,7},{9,8},{8,9},{11,10... | collective-permute-start | bytes 4718600 | tf_op jit(solution)/shard_map/ppermute | solution.py:42
  56.9 21.8 %collective-permute-start.18 = (bf16[128,1536]{1,0:T(8,128)(2,1)S(1)}, bf16[128,1536]{1,0:T(8,128)(2,1)S(1)}, u32[]{:S(2)}, u32[]{:S(2)}) collective-permute-start(bf16[128,1536]{1,0:T(8,128)(2,1)S(1)} %get-tuple-element.43), channel_id=1, source_target_pairs={{0,2},{2,0},{1,3},{3,1},{4,6},{6,4},{5,7},{7,5},{8,10},{10,8},{9,1... | collective-permute-start | bytes 1179656 | tf_op jit(solution)/shard_map/ppermute | solution.py:38
  57.5 27.0 %collective-permute-start.17 = (bf16[128,1536]{1,0:T(8,128)(2,1)S(1)}, bf16[128,1536]{1,0:T(8,128)(2,1)S(1)}, u32[]{:S(2)}, u32[]{:S(2)}) collective-permute-start(bf16[128,1536]{1,0:T(8,128)(2,1)S(1)} %get-tuple-element.42), channel_id=1, source_target_pairs={{0,2},{2,0},{1,3},{3,1},{4,6},{6,4},{5,7},{7,5},{8,10},{10,8},{9,1... | collective-permute-start | bytes 1179656 | tf_op jit(solution)/shard_map/ppermute | solution.py:38
  64.2 26.2 %collective-permute-start.16 = (bf16[128,1536]{1,0:T(8,128)(2,1)S(1)}, bf16[128,1536]{1,0:T(8,128)(2,1)S(1)}, u32[]{:S(2)}, u32[]{:S(2)}) collective-permute-start(bf16[128,1536]{1,0:T(8,128)(2,1)S(1)} %get-tuple-element.41), channel_id=1, source_target_pairs={{0,2},{2,0},{1,3},{3,1},{4,6},{6,4},{5,7},{7,5},{8,10},{10,8},{9,1... | collective-permute-start | bytes 1179656 | tf_op jit(solution)/shard_map/ppermute | solution.py:38
  70.2 28.6 %collective-permute-start.15 = (bf16[128,1536]{1,0:T(8,128)(2,1)S(1)}, bf16[128,1536]{1,0:T(8,128)(2,1)S(1)}, u32[]{:S(2)}, u32[]{:S(2)}) collective-permute-start(bf16[128,1536]{1,0:T(8,128)(2,1)S(1)} %get-tuple-element.40), channel_id=1, source_target_pairs={{0,2},{2,0},{1,3},{3,1},{4,6},{6,4},{5,7},{7,5},{8,10},{10,8},{9,1... | collective-permute-start | bytes 1179656 | tf_op jit(solution)/shard_map/ppermute | solution.py:38
  71.7 1.2 %copy-start.4 = (bf16[128,6144]{1,0:T(8,128)(2,1)}, bf16[128,6144]{1,0:T(8,128)(2,1)S(1)}, u32[]{:S(2)}) copy-start(bf16[128,6144]{1,0:T(8,128)(2,1)S(1)} %collective-permute-done.21.refs_3_) | copy-start | bytes 4718596
  90.4 6.0 %copy-start = (f32[128,6144]{1,0:T(8,128)S(1)}, f32[128,6144]{1,0:T(8,128)}, u32[]{:S(2)}) copy-start(f32[128,6144]{1,0:T(8,128)} %slopes.1.refs_18_.refs_0_) | copy-start | bytes 9437188

commit v3 on v2

--- a/solution.py
+++ b/solution.py
@@ -13,12 +13,12 @@
 bf16 = jnp.bfloat16
 
 LANES = 128
-WEIGHT_CUTS = (1, 1, 1, 1)
+WEIGHT_CUTS = (1,)
 PARTIAL_CUTS = (1, 1, 1, 1)
 TILE = 896
-VMEM = 48 * 2**20
+VMEM = 40 * 2**20
 PARTIAL_COST = 0.01
-WEIGHT_COST = 0.1
+LAST_COST = 0.1
 ANY = pl.BlockSpec(memory_space=pl.ANY)
 
 
@@ -151,37 +151,61 @@
     )[0]
 
 
-def tokens_first(grads_ref, others, weight_ref, weights, half):
-    dims = (((1,), (1,)), ((), ()))
-    product = lax.dot_general(
-        grads_ref[:half], weight_ref[...], dims, preferred_element_type=f32
-    )
-    for other, rows in zip(others, weights):
-        product = product + lax.dot_general(
-            other[...], rows[...], dims, preferred_element_type=f32
-        )
-    return product
-
-
-def partial_products(grads, others, weight, weights, offset, size, block, after):
-    half, width = others[0].shape if others else grads.shape
+def in_order(pieces, place_of, half, tokens):
+    rows, width = pieces[0][0].shape
+    parts = [part for piece in pieces for part in piece]
+    entries, held = len(pieces[0]), rows * len(pieces)
+
+    def kernel(*refs):
+        first_ref, second_ref = refs[-2:]
+        for j in range(len(pieces)):
+            for s in range(entries):
+                part, row = refs[j * entries + s], place_of(s) * held
+
+                @pl.when(row < half)
+                def _():
+                    first_ref[pl.ds(pl.multiple_of(row + j * rows, rows), rows)] = part[...]
+
+                @pl.when(row >= half)
+                def _():
+                    at = pl.multiple_of(row - half + j * rows, rows)
+                    second_ref[pl.ds(at, rows)] = part[...]
+
+    shapes = [(half, width), (tokens - half, width)]
+    return call(
+        kernel,
+        "in_order",
+        (1,),
+        parts,
+        [fixed((rows, width))] * len(parts),
+        [jax.ShapeDtypeStruct(shape, bf16) for shape in shapes],
+        [fixed(shape) for shape in shapes],
+    )
+
+
+def partial_products(grads, weights, offset, size, block, after):
+    half, width = grads[0].shape
     tile = tile_of(offset, size)
     start = offset // tile
-    count = len(others)
-
-    def kernel(grads_ref, weight_ref, *refs):
+    count = len(grads)
+
+    def kernel(*refs):
         own_ref, send_ref = refs[-2:]
-        product = tokens_first(grads_ref, refs[:count], weight_ref, refs[count:-2], half)
+        product = 0.0
+        for part, rows in zip(refs[:count], refs[count:-2]):
+            product = product + lax.dot_general(
+                part[...], rows[...], (((1,), (1,)), ((), ())), preferred_element_type=f32
+            )
         own_ref[...] = product[:block]
         send_ref[...] = product[block:].astype(bf16)
 
-    spec = pl.BlockSpec((tile, width), lambda i: (start + i, 0))
     return call(
         kernel,
         "partial_products",
         (size // tile,),
-        [grads, weight, *others, *weights],
-        [fixed((half, width)), spec] + [fixed((half, width))] * count + [spec] * count,
+        [*grads, *weights],
+        [fixed((half, width))] * count
+        + [pl.BlockSpec((tile, width), lambda i: (start + i, 0))] * count,
         [
             jax.ShapeDtypeStruct((block, size), f32),
             jax.ShapeDtypeStruct((half - block, size), bf16),
@@ -192,70 +216,19 @@
     )
 
 
-def first_products(pieces, other_pieces, place_of, weight, weights, size, block, half, tokens, after):
-    tile = tile_of(0, size)
-    rows, width = pieces[0][0].shape
-    groups = [pieces] + other_pieces
-    parts = [part for group in groups for piece in group for part in piece]
-    split, entries, count = len(pieces), len(pieces[0]), len(other_pieces)
-    held = rows * split
-
-    def kernel(*refs):
-        weight_ref, *refs_of = refs[len(parts) : len(parts) + 1 + count]
-        outs = refs[len(parts) + 1 + count :]
-        grads_ref, other_refs, own_ref, send_ref = outs[0], outs[1:-2], outs[-2], outs[-1]
-
-        @pl.when(pl.program_id(0) == 0)
-        def _():
-            for j in range(split):
-                for s in range(entries):
-                    place = place_of(s)
-                    at = pl.multiple_of(place * held + j * rows, rows)
-                    grads_ref[pl.ds(at, rows)] = refs[j * entries + s][...]
-
-                    @pl.when(place * held < half)
-                    def _():
-                        for k, other in enumerate(other_refs):
-                            source = refs[((k + 1) * split + j) * entries + s]
-                            other[pl.ds(at, rows)] = source[...]
-
-        product = tokens_first(grads_ref, other_refs, weight_ref, refs_of, half)
-        own_ref[...] = product[:block]
-        send_ref[...] = product[block:].astype(bf16)
-
-    spec = pl.BlockSpec((tile, width), lambda i: (i, 0))
-    grads, *rest = call(
-        kernel,
-        "first_products",
-        (size // tile,),
-        parts + [weight, *weights],
-        [fixed((rows, width))] * len(parts) + [spec] * (1 + count),
-        [jax.ShapeDtypeStruct((tokens, width), bf16)]
-        + [jax.ShapeDtypeStruct((half, width), bf16)] * count
-        + [
-            jax.ShapeDtypeStruct((block, size), f32),
-            jax.ShapeDtypeStruct((half - block, size), bf16),
-        ],
-        [fixed((tokens, width))]
-        + [fixed((half, width))] * count
-        + [columns(block, tile), columns(half - block, tile)],
-        after,
-        flops=int(PARTIAL_COST * 2 * 2 * half * width * size),
-    )
-    return grads, rest[:-2], rest[-2], rest[-1]
-
-
 def weight_products(blocks, grads, into, offset, size, scale, after):
-    tokens, width = grads.shape
+    width = grads[0].shape[1]
     block, features = blocks[0].shape
+    count = len(blocks)
     tile = tile_of(offset, size)
     start = offset // tile
 
     def kernel(*refs):
-        grads_ref, out_ref = refs[-2:]
-        hidden = jnp.concatenate([ref[...] for ref in refs[:-2]], axis=0)
+        out_ref = refs[-1]
+        hidden = jnp.concatenate([ref[...] for ref in refs[:count]], axis=0)
+        rows = jnp.concatenate([ref[...] for ref in refs[count:-1]], axis=0)
         product = lax.dot_general(
-            hidden, grads_ref[...], (((0,), (0,)), ((), ())), preferred_element_type=f32
+            hidden, rows, (((0,), (0,)), ((), ())), preferred_element_type=f32
         )
         out_ref[...] = (product * scale).astype(bf16)
 
@@ -263,13 +236,13 @@
         kernel,
         "weight_products",
         (size // tile,),
-        blocks + [grads],
-        [columns(block, tile, start)] * len(blocks) + [fixed((tokens, width))],
+        [*blocks, *grads],
+        [columns(block, tile, start)] * count + [fixed(part.shape) for part in grads],
         [jax.ShapeDtypeStruct((features, width), bf16)],
         [pl.BlockSpec((tile, width), lambda i: (start + i, 0))],
         after,
         into,
-        int(WEIGHT_COST * 2 * tokens * width * size),
+        1024,
     )[0]
 
 
@@ -295,6 +268,7 @@
         [columns(block, tile, offset // tile)],
         after,
         into,
+        int(LAST_COST * 2**20 * size),
     )[0]
 
 
@@ -311,7 +285,7 @@
         ring = rows <= 4
 
         hidden = [hidden_part(preact, 0, features, [])]
-        parts = split_rows(out_grad, 2 if ring else 1, [hidden[0]])
+        parts = split_rows(out_grad, 2 if ring else 1, [])
         hidden += [from_next(hidden[0], "col", cols, dx) for dx in range(1, cols)]
         slope = slopes(preact, [hidden[0]])
 
@@ -320,8 +294,6 @@
             for hop in range(rows - 1):
                 for piece in pieces:
                     piece.append(to_next(piece[-1], "row", rows, 1))
-                if hop == 0:
-                    pieces[-1][-1], slope = lax.optimization_barrier((pieces[-1][-1], slope))
         else:
             whole = lax.all_gather(parts[0], "row", axis=0, tiled=False)
             z = lax.axis_index("row")
@@ -340,28 +312,18 @@
             return (dd * cols + dx) * per_block + lax.rem(row, per_block)
 
         hops = range(1, depths)
-        weights = [from_next(weight, "depth", depths, dd) for dd in hops]
-        if ring:
-            for piece in pieces:
-                *piece[:-1], _ = lax.optimization_barrier((*piece[:-1], pieces[-1][-2]))
-        other_pieces = [
-            [[from_next(part, "depth", depths, dd) for part in piece] for piece in pieces]
-            for dd in hops
+        first, second = in_order(pieces, place_of, half, tokens)
+        weights = [weight] + [from_next(weight, "depth", depths, dd) for dd in hops]
+        grads = [first] + [
+            to_next(second[(dd - 1) * half : dd * half], "depth", depths, dd) for dd in hops
         ]
 
         chunks = cut(features, PARTIAL_CUTS)
         count = len(chunks)
         owns, far = [], []
         for c, (offset, size) in enumerate(chunks):
-            if c == 0:
-                grads, others, own, send = first_products(
-                    pieces, other_pieces, place_of, weight, weights, size, block, half, tokens,
-                    [slope],
-                )
-            else:
-                own, send = partial_products(
-                    grads, others, weight, weights, offset, size, block, owns[-1:]
-                )
+            after = owns[-1:] if owns else [slope]
+            own, send = partial_products(grads, weights, offset, size, block, after)
             owns.append(own)
             far.append(
                 [
@@ -370,12 +332,14 @@
                 ]
             )
 
-        *blocks, _ = lax.optimization_barrier((*hidden, owns[min(1, count - 1)]))
+        *blocks, _ = lax.optimization_barrier((*hidden, owns[0]))
         blocks += [from_next(part, "depth", depths, dd) for dd in hops for part in blocks]
         weight_grad = None
         for k, (offset, size) in enumerate(cut(features, WEIGHT_CUTS)):
-            after = owns[-1:] if k == 0 else far[k - 1][-1:] if k < count else []
-            weight_grad = weight_products(blocks, grads, weight_grad, offset, size, scale, after)
+            after = owns[-1:] if k == 0 else far[k - 1][-1:]
+            weight_grad = weight_products(
+                blocks, [first, second], weight_grad, offset, size, scale, after
+            )
         preact_grad = None
         for c in range(count):
             preact_grad = last_step(

time: 100 us -> 83.5 us (0.83)
  Pallas kernels: 54.1 us -> 41.9 us
  starting transfers between devices: 14.3 us -> 11.5 us
  local copies, waits for them, and re-layouts: 4.01 us -> 1.42 us
  waiting for transfers between devices: 26.6 us -> 27.8 us
    pallas_call x15 -> x13, Pallas kernels: 54.1 us -> 41.9 us  [call(): pl.pallas_call(body, grid=grid, in_specs=list(in_specs) + [ANY] * len(ext...]
    ppermute x10 -> x11, waiting for transfers between devices: 23.9 us -> 27.8 us  [to_next(): lax.ppermute(array, axis, [(i, (i + hop) % size) for i in range(size)])]
    ppermute x12 -> x4, waiting for transfers between devices: 2.63 us -> 0.01 us  [from_next(): lax.ppermute(array, axis, [((i + hop) % size, i) for i in range(size)])]
    unnamed x10 -> x6, local copies, waits for them, and re-layouts: 4.01 us -> 1.42 us
    ppermute x12 -> x4, starting transfers between devices: 5.22 us -> 3.71 us  [from_next(): lax.ppermute(array, axis, [((i + hop) % size, i) for i in range(size)])]
    ppermute x10 -> x11, starting transfers between devices: 9.04 us -> 7.81 us  [to_next(): lax.ppermute(array, axis, [(i, (i + hop) % size) for i in range(size)])]
  transfers between devices with their start and end apart: 22 -> 15, of which waited for: 8 -> 7; matrix products, arithmetic and copies ran while one was open for 0% -> 0% of each run, Pallas kernels for 53% -> 49%
where the time goes in v3:
time: 83.5 us; the launch traced here: 83.4 us
  Pallas kernels  41.9 us (50%)
  waiting for transfers between devices  27.8 us (33%)
  starting transfers between devices  11.5 us (14%)
  local copies, waits for them, and re-layouts  1.42 us (2%)
    pallas_call x13, Pallas kernels, call(): pl.pallas_call(body, grid=grid, in_specs=list(in_specs) + [ANY] * len(ext...  41.9 us
    ppermute x11, waiting for transfers between devices, to_next(): lax.ppermute(array, axis, [(i, (i + hop) % size) for i in range(size)])  27.8 us
    ppermute x11, starting transfers between devices, to_next(): lax.ppermute(array, axis, [(i, (i + hop) % size) for i in range(size)])  7.81 us
    ppermute x4, starting transfers between devices, from_next(): lax.ppermute(array, axis, [((i + hop) % size, i) for i in range(size)])  3.71 us
  transfers between devices with their start and end apart: 15, of which 7 were waited for; matrix products, arithmetic and copies ran while one was open for 0% of the time, Pallas kernels for 49%

profile of v3, /device:TPU:0, one launch (start us, length us, event | category | flops | bytes accessed | tf_op | source)
XLA Modules:
  0.0 83.4 jit_solution(16138572061356226121)
XLA Ops:
  0.6 0.5 collective-permute-start.7
  1.1 0.0 copy-start
  1.1 1.4 %copy-done = bf16[128,6144]{1,0:T(8,128)(2,1)S(1)} copy-done((bf16[128,6144]{1,0:T(8,128)(2,1)S(1)}, bf16[128,6144]{1,0:T(8,128)(2,1)}, u32[]{:S(2)}) %copy-start) | copy-done | bytes 1572888
  2.6 0.0 copy-start.2
  2.6 1.4 %hidden_part.1.refs_1_.refs_0_ = bf16[128,6144]{1,0:T(8,128)(2,1)S(1)} custom-call(bf16[128,6144]{1,0:T(8,128)(2,1)S(1)} %copy-done), custom_call_target="tpu_custom_call" | custom-call | bytes 1024 | tf_op jit(solution)/shard_map/hidden_part/pallas_call | solution.py:72
  4.0 0.0 copy-start.1
  4.0 2.6 %collective-permute-start.12 = (bf16[128,6144]{1,0:T(8,128)(2,1)S(1)}, bf16[128,6144]{1,0:T(8,128)(2,1)S(1)}, u32[]{:S(2)}, u32[]{:S(2)}) collective-permute-start(bf16[128,6144]{1,0:T(8,128)(2,1)S(1)} %hidden_part.1.refs_1_.refs_0_), channel_id=1, source_target_pairs={{2,0},{0,2},{3,1},{1,3},{6,4},{4,6},{7,5},{5,7},{10,8},{8,10},{11,... | collective-permute-start | bytes 4718600 | tf_op jit(solution)/shard_map/ppermute | solution.py:42
  6.6 0.0 copy-done.2
  6.6 1.6 %collective-permute-start = (bf16[64,1536]{1,0:T(8,128)(2,1)S(1)}, bf16[64,1536]{1,0:T(8,128)(2,1)S(1)}, u32[]{:S(2)}, u32[]{:S(2)}) collective-permute-start(bf16[64,1536]{1,0:T(8,128)(2,1)S(1)} %get-tuple-element.16.refs_0_), channel_id=1, source_target_pairs={{0,4},{4,8},{8,12},{12,0},{1,5},{5,9},{9,13},{13,1},{2,6},{6,10},{... | collective-permute-start | bytes 589832 | tf_op jit(solution)/shard_map/ppermute | solution.py:38
  8.2 1.6 %collective-permute-start.3 = (bf16[64,1536]{1,0:T(8,128)(2,1)S(1)}, bf16[64,1536]{1,0:T(8,128)(2,1)S(1)}, u32[]{:S(2)}, u32[]{:S(2)}) collective-permute-start(bf16[64,1536]{1,0:T(8,128)(2,1)S(1)} %get-tuple-element.17.refs_4_), channel_id=1, source_target_pairs={{0,4},{4,8},{8,12},{12,0},{1,5},{5,9},{9,13},{13,1},{2,6},{6,10},{... | collective-permute-start | bytes 589832 | tf_op jit(solution)/shard_map/ppermute | solution.py:38
  9.8 6.4 %collective-permute-done.refs_1_ = bf16[64,1536]{1,0:T(8,128)(2,1)S(1)} collective-permute-done((bf16[64,1536]{1,0:T(8,128)(2,1)S(1)}, bf16[64,1536]{1,0:T(8,128)(2,1)S(1)}, u32[]{:S(2)}, u32[]{:S(2)}) %collective-permute-start) | collective-permute-done | bytes 196640 | tf_op jit(solution)/shard_map/ppermute | solution.py:38
  16.2 0.0 collective-permute-start.1
  16.2 3.9 %collective-permute-done.3.refs_5_ = bf16[64,1536]{1,0:T(8,128)(2,1)S(1)} collective-permute-done((bf16[64,1536]{1,0:T(8,128)(2,1)S(1)}, bf16[64,1536]{1,0:T(8,128)(2,1)S(1)}, u32[]{:S(2)}, u32[]{:S(2)}) %collective-permute-start.3) | collective-permute-done | bytes 196640 | tf_op jit(solution)/shard_map/ppermute | solution.py:38
  20.0 0.1 collective-permute-start.4
  20.2 4.1 %collective-permute-done.1.refs_2_ = bf16[64,1536]{1,0:T(8,128)(2,1)S(1)} collective-permute-done((bf16[64,1536]{1,0:T(8,128)(2,1)S(1)}, bf16[64,1536]{1,0:T(8,128)(2,1)S(1)}, u32[]{:S(2)}, u32[]{:S(2)}) %collective-permute-start.1) | collective-permute-done | bytes 196640 | tf_op jit(solution)/shard_map/ppermute | solution.py:38
  24.2 0.1 collective-permute-start.2
  24.4 5.3 %collective-permute-done.4.refs_6_ = bf16[64,1536]{1,0:T(8,128)(2,1)S(1)} collective-permute-done((bf16[64,1536]{1,0:T(8,128)(2,1)S(1)}, bf16[64,1536]{1,0:T(8,128)(2,1)S(1)}, u32[]{:S(2)}, u32[]{:S(2)}) %collective-permute-start.4) | collective-permute-done | bytes 196640 | tf_op jit(solution)/shard_map/ppermute | solution.py:38
  29.7 0.0 collective-permute-start.5
  29.7 3.9 %collective-permute-done.2.refs_3_ = bf16[64,1536]{1,0:T(8,128)(2,1)S(1)} collective-permute-done((bf16[64,1536]{1,0:T(8,128)(2,1)S(1)}, bf16[64,1536]{1,0:T(8,128)(2,1)S(1)}, u32[]{:S(2)}, u32[]{:S(2)}) %collective-permute-start.2) | collective-permute-done | bytes 196640 | tf_op jit(solution)/shard_map/ppermute | solution.py:38
  33.5 3.6 %collective-permute-done.5.refs_7_ = bf16[64,1536]{1,0:T(8,128)(2,1)S(1)} collective-permute-done((bf16[64,1536]{1,0:T(8,128)(2,1)S(1)}, bf16[64,1536]{1,0:T(8,128)(2,1)S(1)}, u32[]{:S(2)}, u32[]{:S(2)}) %collective-permute-start.5) | collective-permute-done | bytes 196640 | tf_op jit(solution)/shard_map/ppermute | solution.py:38
  37.1 0.2 in_order.1
  37.3 0.1 collective-permute-start.6
  37.4 0.0 copy-done.1
  37.4 2.4 %slopes.1.refs_4_.refs_0_ = f32[128,6144]{1,0:T(8,128)S(1)} custom-call(bf16[128,6144]{1,0:T(8,128)(2,1)S(1)} %copy-done.1, bf16[128,6144]{1,0:T(8,128)(2,1)S(1)} %hidden_part.1.refs_1_.refs_0_), custom_call_target="tpu_custom_call" | custom-call | bytes 1024 | tf_op jit(solution)/shard_map/slopes/pallas_call | solution.py:72
  39.8 0.0 collective-permute-done.6.refs_1_
  39.8 0.0 collective-permute-done.7.refs_3_
  39.8 5.3 %partial_products.4 = (f32[128,1536]{1,0:T(8,128)S(1)}, bf16[128,1536]{1,0:T(8,128)(2,1)S(1)}) custom-call(bf16[256,1536]{1,0:T(8,128)(2,1)S(1)} %get-tuple-element.18.refs_0_.refs_4_, bf16[256,1536]{1,0:T(8,128)(2,1)S(1)} %collective-permute-done.6.refs_1_, bf16[6144,1536]{1,0:T(8,128)(2,1)} %refs_2_.7, bf16[6144,1536]{1,0:T(8,128)(2,1)} %collective-permute-done.7.refs_3_, ...), custom_call_target="tpu_custom_call" | custom-call | flops 24159192 | bytes 1024 | tf_op jit(solution)/shard_map/partial_products/pallas_call | solution.py:72
  45.2 0.0 collective-permute-done.12.refs_1_
  45.2 0.5 collective-permute-start.13
  45.7 0.1 collective-permute-start.14
  45.8 0.3 collective-permute-start.11
  46.0 5.3 %partial_products.5 = (f32[128,1536]{1,0:T(8,128)S(1)}, bf16[128,1536]{1,0:T(8,128)(2,1)S(1)}) custom-call(bf16[256,1536]{1,0:T(8,128)(2,1)S(1)} %get-tuple-element.18.refs_0_.refs_4_, bf16[256,1536]{1,0:T(8,128)(2,1)S(1)} %collective-permute-done.6.refs_1_, bf16[6144,1536]{1,0:T(8,128)(2,1)} %refs_2_.7, bf16[6144,1536]{1,0:T(8,128)(2,1)} %collective-permute-done.7.refs_3_, ...), custom_call_target="tpu_custom_call" | custom-call | flops 24159192 | bytes 1024 | tf_op jit(solution)/shard_map/partial_products/pallas_call | solution.py:72
  51.3 1.8 %collective-permute-start.10 = (bf16[128,1536]{1,0:T(8,128)(2,1)S(1)}, bf16[128,1536]{1,0:T(8,128)(2,1)S(1)}, u32[]{:S(2)}, u32[]{:S(2)}) collective-permute-start(bf16[128,1536]{1,0:T(8,128)(2,1)S(1)} %get-tuple-element.26), channel_id=1, source_target_pairs={{0,2},{2,0},{1,3},{3,1},{4,6},{6,4},{5,7},{7,5},{8,10},{10,8},{9,1... | collective-permute-start | bytes 1179656 | tf_op jit(solution)/shard_map/ppermute | solution.py:38
  53.2 5.3 %partial_products.6 = (f32[128,1536]{1,0:T(8,128)S(1)}, bf16[128,1536]{1,0:T(8,128)(2,1)S(1)}) custom-call(bf16[256,1536]{1,0:T(8,128)(2,1)S(1)} %get-tuple-element.18.refs_0_.refs_4_, bf16[256,1536]{1,0:T(8,128)(2,1)S(1)} %collective-permute-done.6.refs_1_, bf16[6144,1536]{1,0:T(8,128)(2,1)} %refs_2_.7, bf16[6144,1536]{1,0:T(8,128)(2,1)} %collective-permute-done.7.refs_3_, ...), custom_call_target="tpu_custom_call" | custom-call | flops 24159192 | bytes 1024 | tf_op jit(solution)/shard_map/partial_products/pallas_call | solution.py:72
  58.5 0.3 collective-permute-start.9
  58.8 5.3 %partial_products.7 = (f32[128,1536]{1,0:T(8,128)S(1)}, bf16[128,1536]{1,0:T(8,128)(2,1)S(1)}) custom-call(bf16[256,1536]{1,0:T(8,128)(2,1)S(1)} %get-tuple-element.18.refs_0_.refs_4_, bf16[256,1536]{1,0:T(8,128)(2,1)S(1)} %collective-permute-done.6.refs_1_, bf16[6144,1536]{1,0:T(8,128)(2,1)} %refs_2_.7, bf16[6144,1536]{1,0:T(8,128)(2,1)} %collective-permute-done.7.refs_3_, ...), custom_call_target="tpu_custom_call" | custom-call | flops 24159192 | bytes 1024 | tf_op jit(solution)/shard_map/partial_products/pallas_call | solution.py:72
  64.1 0.0 collective-permute-done.13.refs_2_
  64.1 1.8 %collective-permute-start.8 = (bf16[128,1536]{1,0:T(8,128)(2,1)S(1)}, bf16[128,1536]{1,0:T(8,128)(2,1)S(1)}, u32[]{:S(2)}, u32[]{:S(2)}) collective-permute-start(bf16[128,1536]{1,0:T(8,128)(2,1)S(1)} %get-tuple-element.24), channel_id=1, source_target_pairs={{0,2},{2,0},{1,3},{3,1},{4,6},{6,4},{5,7},{7,5},{8,10},{10,8},{9,1... | collective-permute-start | bytes 1179656 | tf_op jit(solution)/shard_map/ppermute | solution.py:38
  66.0 0.0 collective-permute-done.14.refs_3_
  66.0 13.3 %weight_products.1.refs_3_ = bf16[6144,1536]{1,0:T(8,128)(2,1)} custom-call(bf16[128,6144]{1,0:T(8,128)(2,1)S(1)} %hidden_part.1.refs_1_.refs_0_, bf16[128,6144]{1,0:T(8,128)(2,1)S(1)} %collective-permute-done.12.refs_1_, bf16[128,6144]{1,0:T(8,128)(2,1)S(1)} %collective-permute-done.13.refs_2_, bf16[128,6144]{1,0:T(8,128)(2,1)S(1)} %collective-permute-done.14.refs_3_, ...), custom_call_target="tpu_custom_call" | custom-call | flops 1024 | bytes 1024 | tf_op jit(solution)/shard_map/weight_products/pallas_call | solution.py:72
  79.3 0.0 collective-permute-done.11.refs_2_
  79.3 0.8 %last_step.4.refs_3_ = bf16[128,6144]{1,0:T(8,128)(2,1)} custom-call(f32[128,6144]{1,0:T(8,128)S(1)} %slopes.1.refs_4_.refs_0_, f32[128,1536]{1,0:T(8,128)S(1)} %get-tuple-element.20.refs_4_.refs_1_, bf16[128,1536]{1,0:T(8,128)(2,1)S(1)} %collective-permute-done.11.refs_2_, bf16[6144,1536]{1,0:T(8,128)(2,1)} %weight_products.1.refs_3_), custom_call_target="tpu_custom_call" | custom-call | flops 161061280 | bytes 1024 | tf_op jit(solution)/shard_map/last_step/pallas_call | solution.py:72
  80.1 0.0 collective-permute-done.10.refs_2_
  80.1 0.8 %last_step.5.refs_3_ = bf16[128,6144]{1,0:T(8,128)(2,1)} custom-call(f32[128,6144]{1,0:T(8,128)S(1)} %slopes.1.refs_4_.refs_0_, f32[128,1536]{1,0:T(8,128)S(1)} %get-tuple-element.21.refs_4_.refs_1_, bf16[128,1536]{1,0:T(8,128)(2,1)S(1)} %collective-permute-done.10.refs_2_, bf16[128,6144]{1,0:T(8,128)(2,1)} %last_step.4.refs_3_), custom_call_target="tpu_custom_call", output_to_operand_aliasing={{}: (3, {})} | custom-call | flops 161061280 | bytes 1024 | tf_op jit(solution)/shard_map/last_step/pallas_call | solution.py:72
  81.0 0.0 collective-permute-done.9.refs_2_
  81.0 0.8 %last_step.6.refs_3_ = bf16[128,6144]{1,0:T(8,128)(2,1)} custom-call(f32[128,6144]{1,0:T(8,128)S(1)} %slopes.1.refs_4_.refs_0_, f32[128,1536]{1,0:T(8,128)S(1)} %get-tuple-element.22.refs_4_.refs_1_, bf16[128,1536]{1,0:T(8,128)(2,1)S(1)} %collective-permute-done.9.refs_2_, bf16[128,6144]{1,0:T(8,128)(2,1)} %last_step.5.refs_3_), custom_call_target="tpu_custom_call", output_to_operand_aliasing={{}: (3, {})} | custom-call | flops 161061280 | bytes 1024 | tf_op jit(solution)/shard_map/last_step/pallas_call | solution.py:72
  81.8 0.7 collective-permute-done.8.refs_2_
  82.5 0.8 %last_step.7 = bf16[128,6144]{1,0:T(8,128)(2,1)} custom-call(f32[128,6144]{1,0:T(8,128)S(1)} %slopes.1.refs_4_.refs_0_, f32[128,1536]{1,0:T(8,128)S(1)} %get-tuple-element.23.refs_6_.refs_1_, bf16[128,1536]{1,0:T(8,128)(2,1)S(1)} %collective-permute-done.8.refs_2_, bf16[128,6144]{1,0:T(8,128)(2,1)} %last_step.6.refs_3_), custom_call_target="tpu_custom_call", output_to_operand_aliasing={{}: (3, {})} | custom-call | flops 161061280 | bytes 1024 | tf_op jit(solution)/shard_map/last_step/pallas_call | solution.py:72
  (1 shorter events, 0.0 us)
Async XLA Ops:
  0.6 39.2 %collective-permute-start.7 = (bf16[6144,1536]{1,0:T(8,128)(2,1)}, bf16[6144,1536]{1,0:T(8,128)(2,1)}, u32[]{:S(2)}, u32[]{:S(2)}) collective-permute-start(bf16[6144,1536]{1,0:T(8,128)(2,1)} %refs_2_.7), channel_id=1, source_target_pairs={{1,0},{0,1},{3,2},{2,3},{5,4},{4,5},{7,6},{6,7},{9,8},{8,9},{11,10... | collective-permute-start | bytes 56623112 | tf_op jit(solution)/shard_map/ppermute | solution.py:42
  1.1 1.4 %copy-start = (bf16[128,6144]{1,0:T(8,128)(2,1)S(1)}, bf16[128,6144]{1,0:T(8,128)(2,1)}, u32[]{:S(2)}) copy-start(bf16[128,6144]{1,0:T(8,128)(2,1)} %refs_0_.4) | copy-start | bytes 4718596
  2.6 4.0 %copy-start.2 = (bf16[128,1536]{1,0:T(8,128)(2,1)S(1)}, bf16[128,1536]{1,0:T(8,128)(2,1)}, u32[]{:S(2)}) copy-start(bf16[128,1536]{1,0:T(8,128)(2,1)} %refs_0_.5) | copy-start | bytes 1179652
  4.0 33.4 %copy-start.1 = (bf16[128,6144]{1,0:T(8,128)(2,1)S(1)}, bf16[128,6144]{1,0:T(8,128)(2,1)}, u32[]{:S(2)}) copy-start(bf16[128,6144]{1,0:T(8,128)(2,1)} %refs_0_.4) | copy-start | bytes 4718596
  4.0 41.2 %collective-permute-start.12 = (bf16[128,6144]{1,0:T(8,128)(2,1)S(1)}, bf16[128,6144]{1,0:T(8,128)(2,1)S(1)}, u32[]{:S(2)}, u32[]{:S(2)}) collective-permute-start(bf16[128,6144]{1,0:T(8,128)(2,1)S(1)} %hidden_part.1.refs_1_.refs_0_), channel_id=1, source_target_pairs={{2,0},{0,2},{3,1},{1,3},{6,4},{4,6},{7,5},{5,7},{10,8},{8,10},{11,... | collective-permute-start | bytes 4718600 | tf_op jit(solution)/shard_map/ppermute | solution.py:42
  6.6 9.6 %collective-permute-start = (bf16[64,1536]{1,0:T(8,128)(2,1)S(1)}, bf16[64,1536]{1,0:T(8,128)(2,1)S(1)}, u32[]{:S(2)}, u32[]{:S(2)}) collective-permute-start(bf16[64,1536]{1,0:T(8,128)(2,1)S(1)} %get-tuple-element.16.refs_0_), channel_id=1, source_target_pairs={{0,4},{4,8},{8,12},{12,0},{1,5},{5,9},{9,13},{13,1},{2,6},{6,10},{... | collective-permute-start | bytes 589832 | tf_op jit(solution)/shard_map/ppermute | solution.py:38
  8.2 11.8 %collective-permute-start.3 = (bf16[64,1536]{1,0:T(8,128)(2,1)S(1)}, bf16[64,1536]{1,0:T(8,128)(2,1)S(1)}, u32[]{:S(2)}, u32[]{:S(2)}) collective-permute-start(bf16[64,1536]{1,0:T(8,128)(2,1)S(1)} %get-tuple-element.17.refs_4_), channel_id=1, source_target_pairs={{0,4},{4,8},{8,12},{12,0},{1,5},{5,9},{9,13},{13,1},{2,6},{6,10},{... | collective-permute-start | bytes 589832 | tf_op jit(solution)/shard_map/ppermute | solution.py:38
  16.2 8.1 %collective-permute-start.1 = (bf16[64,1536]{1,0:T(8,128)(2,1)S(1)}, bf16[64,1536]{1,0:T(8,128)(2,1)S(1)}, u32[]{:S(2)}, u32[]{:S(2)}) collective-permute-start(bf16[64,1536]{1,0:T(8,128)(2,1)S(1)} %collective-permute-done.refs_1_), channel_id=1, source_target_pairs={{0,4},{4,8},{8,12},{12,0},{1,5},{5,9},{9,13},{13,1},{2,6},{6,10},{... | collective-permute-start | bytes 589832 | tf_op jit(solution)/shard_map/ppermute | solution.py:38
  20.0 9.6 %collective-permute-start.4 = (bf16[64,1536]{1,0:T(8,128)(2,1)S(1)}, bf16[64,1536]{1,0:T(8,128)(2,1)S(1)}, u32[]{:S(2)}, u32[]{:S(2)}) collective-permute-start(bf16[64,1536]{1,0:T(8,128)(2,1)S(1)} %collective-permute-done.3.refs_5_), channel_id=1, source_target_pairs={{0,4},{4,8},{8,12},{12,0},{1,5},{5,9},{9,13},{13,1},{2,6},{6,10},{... | collective-permute-start | bytes 589832 | tf_op jit(solution)/shard_map/ppermute | solution.py:38
  24.2 9.3 %collective-permute-start.2 = (bf16[64,1536]{1,0:T(8,128)(2,1)S(1)}, bf16[64,1536]{1,0:T(8,128)(2,1)S(1)}, u32[]{:S(2)}, u32[]{:S(2)}) collective-permute-start(bf16[64,1536]{1,0:T(8,128)(2,1)S(1)} %collective-permute-done.1.refs_2_), channel_id=1, source_target_pairs={{0,4},{4,8},{8,12},{12,0},{1,5},{5,9},{9,13},{13,1},{2,6},{6,10},{... | collective-permute-start | bytes 589832 | tf_op jit(solution)/shard_map/ppermute | solution.py:38
  29.7 7.5 %collective-permute-start.5 = (bf16[64,1536]{1,0:T(8,128)(2,1)S(1)}, bf16[64,1536]{1,0:T(8,128)(2,1)S(1)}, u32[]{:S(2)}, u32[]{:S(2)}) collective-permute-start(bf16[64,1536]{1,0:T(8,128)(2,1)S(1)} %collective-permute-done.4.refs_6_), channel_id=1, source_target_pairs={{0,4},{4,8},{8,12},{12,0},{1,5},{5,9},{9,13},{13,1},{2,6},{6,10},{... | collective-permute-start | bytes 589832 | tf_op jit(solution)/shard_map/ppermute | solution.py:38
  37.3 2.5 %collective-permute-start.6 = (bf16[256,1536]{1,0:T(8,128)(2,1)S(1)}, bf16[256,1536]{1,0:T(8,128)(2,1)S(1)}, u32[]{:S(2)}, u32[]{:S(2)}) collective-permute-start(bf16[256,1536]{1,0:T(8,128)(2,1)S(1)} %get-tuple-element.19.refs_5_), channel_id=1, source_target_pairs={{0,1},{1,0},{2,3},{3,2},{4,5},{5,4},{6,7},{7,6},{8,9},{9,8},{10,11... | collective-permute-start | bytes 2359304 | tf_op jit(solution)/shard_map/ppermute | solution.py:38
  45.2 19.0 %collective-permute-start.13 = (bf16[128,6144]{1,0:T(8,128)(2,1)S(1)}, bf16[128,6144]{1,0:T(8,128)(2,1)S(1)}, u32[]{:S(2)}, u32[]{:S(2)}) collective-permute-start(bf16[128,6144]{1,0:T(8,128)(2,1)S(1)} %hidden_part.1.refs_1_.refs_0_), channel_id=1, source_target_pairs={{1,0},{0,1},{3,2},{2,3},{5,4},{4,5},{7,6},{6,7},{9,8},{8,9},{11,10... | collective-permute-start | bytes 4718600 | tf_op jit(solution)/shard_map/ppermute | solution.py:42
  45.7 20.3 %collective-permute-start.14 = (bf16[128,6144]{1,0:T(8,128)(2,1)S(1)}, bf16[128,6144]{1,0:T(8,128)(2,1)S(1)}, u32[]{:S(2)}, u32[]{:S(2)}) collective-permute-start(bf16[128,6144]{1,0:T(8,128)(2,1)S(1)} %collective-permute-done.12.refs_1_), channel_id=1, source_target_pairs={{1,0},{0,1},{3,2},{2,3},{5,4},{4,5},{7,6},{6,7},{9,8},{8,9},{11,10... | collective-permute-start | bytes 4718600 | tf_op jit(solution)/shard_map/ppermute | solution.py:42
  45.8 33.5 %collective-permute-start.11 = (bf16[128,1536]{1,0:T(8,128)(2,1)S(1)}, bf16[128,1536]{1,0:T(8,128)(2,1)S(1)}, u32[]{:S(2)}, u32[]{:S(2)}) collective-permute-start(bf16[128,1536]{1,0:T(8,128)(2,1)S(1)} %get-tuple-element.27), channel_id=1, source_target_pairs={{0,2},{2,0},{1,3},{3,1},{4,6},{6,4},{5,7},{7,5},{8,10},{10,8},{9,1... | collective-permute-start | bytes 1179656 | tf_op jit(solution)/shard_map/ppermute | solution.py:38
  51.3 28.8 %collective-permute-start.10 = (bf16[128,1536]{1,0:T(8,128)(2,1)S(1)}, bf16[128,1536]{1,0:T(8,128)(2,1)S(1)}, u32[]{:S(2)}, u32[]{:S(2)}) collective-permute-start(bf16[128,1536]{1,0:T(8,128)(2,1)S(1)} %get-tuple-element.26), channel_id=1, source_target_pairs={{0,2},{2,0},{1,3},{3,1},{4,6},{6,4},{5,7},{7,5},{8,10},{10,8},{9,1... | collective-permute-start | bytes 1179656 | tf_op jit(solution)/shard_map/ppermute | solution.py:38
  58.5 22.5 %collective-permute-start.9 = (bf16[128,1536]{1,0:T(8,128)(2,1)S(1)}, bf16[128,1536]{1,0:T(8,128)(2,1)S(1)}, u32[]{:S(2)}, u32[]{:S(2)}) collective-permute-start(bf16[128,1536]{1,0:T(8,128)(2,1)S(1)} %get-tuple-element.25), channel_id=1, source_target_pairs={{0,2},{2,0},{1,3},{3,1},{4,6},{6,4},{5,7},{7,5},{8,10},{10,8},{9,1... | collective-permute-start | bytes 1179656 | tf_op jit(solution)/shard_map/ppermute | solution.py:38
  64.1 18.4 %collective-permute-start.8 = (bf16[128,1536]{1,0:T(8,128)(2,1)S(1)}, bf16[128,1536]{1,0:T(8,128)(2,1)S(1)}, u32[]{:S(2)}, u32[]{:S(2)}) collective-permute-start(bf16[128,1536]{1,0:T(8,128)(2,1)S(1)} %get-tuple-element.24), channel_id=1, source_target_pairs={{0,2},{2,0},{1,3},{3,1},{4,6},{6,4},{5,7},{7,5},{8,10},{10,8},{9,1... | collective-permute-start | bytes 1179656 | tf_op jit(solution)/shard_map/ppermute | solution.py:38

commit v4 on v3

--- a/solution.py
+++ b/solution.py
@@ -151,7 +151,7 @@
     )[0]
 
 
-def in_order(pieces, place_of, half, tokens):
+def in_order(pieces, place_of, half, tokens, after):
     rows, width = pieces[0][0].shape
     parts = [part for piece in pieces for part in piece]
     entries, held = len(pieces[0]), rows * len(pieces)
@@ -180,6 +180,7 @@
         [fixed((rows, width))] * len(parts),
         [jax.ShapeDtypeStruct(shape, bf16) for shape in shapes],
         [fixed(shape) for shape in shapes],
+        after,
     )
 
 
@@ -216,7 +217,7 @@
     )
 
 
-def weight_products(blocks, grads, into, offset, size, scale, after):
+def weight_products(blocks, cols, grads, into, offset, size, scale, after):
     width = grads[0].shape[1]
     block, features = blocks[0].shape
     count = len(blocks)
@@ -225,7 +226,11 @@
 
     def kernel(*refs):
         out_ref = refs[-1]
-        hidden = jnp.concatenate([ref[...] for ref in refs[:count]], axis=0)
+        hidden = [ref[...] for ref in refs[:count]]
+        for k in range(count):
+            if k % cols:
+                hidden[k] = gelu_value(hidden[k].astype(f32)).astype(bf16)
+        hidden = jnp.concatenate(hidden, axis=0)
         rows = jnp.concatenate([ref[...] for ref in refs[count:-1]], axis=0)
         product = lax.dot_general(
             hidden, rows, (((0,), (0,)), ((), ())), preferred_element_type=f32
@@ -284,9 +289,9 @@
         per_block = block // row_tokens
         ring = rows <= 4
 
-        hidden = [hidden_part(preact, 0, features, [])]
+        arrived = [from_next(preact, "col", cols, dx) for dx in range(1, cols)]
         parts = split_rows(out_grad, 2 if ring else 1, [])
-        hidden += [from_next(hidden[0], "col", cols, dx) for dx in range(1, cols)]
+        hidden = [hidden_part(preact, 0, features, [parts[0]])]
         slope = slopes(preact, [hidden[0]])
 
         if ring:
@@ -312,7 +317,7 @@
             return (dd * cols + dx) * per_block + lax.rem(row, per_block)
 
         hops = range(1, depths)
-        first, second = in_order(pieces, place_of, half, tokens)
+        first, second = in_order(pieces, place_of, half, tokens, [slope])
         weights = [weight] + [from_next(weight, "depth", depths, dd) for dd in hops]
         grads = [first] + [
             to_next(second[(dd - 1) * half : dd * half], "depth", depths, dd) for dd in hops
@@ -322,7 +327,7 @@
         count = len(chunks)
         owns, far = [], []
         for c, (offset, size) in enumerate(chunks):
-            after = owns[-1:] if owns else [slope]
+            after = owns[-1:]
             own, send = partial_products(grads, weights, offset, size, block, after)
             owns.append(own)
             far.append(
@@ -332,13 +337,14 @@
                 ]
             )
 
-        *blocks, _ = lax.optimization_barrier((*hidden, owns[0]))
+        *raw, _ = lax.optimization_barrier((*arrived, owns[0]))
+        blocks = hidden + raw
         blocks += [from_next(part, "depth", depths, dd) for dd in hops for part in blocks]
         weight_grad = None
         for k, (offset, size) in enumerate(cut(features, WEIGHT_CUTS)):
             after = owns[-1:] if k == 0 else far[k - 1][-1:]
             weight_grad = weight_products(
-                blocks, [first, second], weight_grad, offset, size, scale, after
+                blocks, cols, [first, second], weight_grad, offset, size, scale, after
             )
         preact_grad = None
         for c in range(count):

time: 83.5 us -> 81.1 us (0.971)
  waiting for transfers between devices: 27.8 us -> 24 us
  local copies, waits for them, and re-layouts: 1.42 us -> 2.4 us
    ppermute x11, waiting for transfers between devices: 27.8 us -> 24 us  [to_next(): lax.ppermute(array, axis, [(i, (i + hop) % size) for i in range(size)])]
    unnamed x6 -> x4, local copies, waits for them, and re-layouts: 1.42 us -> 2.4 us
  transfers between devices with their start and end apart: 15 -> 15, of which waited for: 7 -> 7; matrix products, arithmetic and copies ran while one was open for 0% -> 0% of each run, Pallas kernels for 49% -> 51%
where the time goes in v4:
time: 81.1 us; the launch traced here: 80.9 us
  Pallas kernels  42.1 us (52%)
  waiting for transfers between devices  24 us (30%)
  starting transfers between devices  11.6 us (14%)
  local copies, waits for them, and re-layouts  2.4 us (3%)
    pallas_call x13, Pallas kernels, call(): pl.pallas_call(body, grid=grid, in_specs=list(in_specs) + [ANY] * len(ext...  42.1 us
    ppermute x11, waiting for transfers between devices, to_next(): lax.ppermute(array, axis, [(i, (i + hop) % size) for i in range(size)])  24 us
    ppermute x11, starting transfers between devices, to_next(): lax.ppermute(array, axis, [(i, (i + hop) % size) for i in range(size)])  7.84 us
    ppermute x4, starting transfers between devices, from_next(): lax.ppermute(array, axis, [((i + hop) % size, i) for i in range(size)])  3.79 us
    unnamed x4, local copies, waits for them, and re-layouts  2.4 us
  transfers between devices with their start and end apart: 15, of which 7 were waited for; matrix products, arithmetic and copies ran while one was open for 0% of the time, Pallas kernels for 51%

profile of v4, /device:TPU:0, one launch (start us, length us, event | category | flops | bytes accessed | tf_op | source)
XLA Modules:
  0.0 80.9 jit_solution(18092071669242932126)
XLA Ops:
  0.6 0.5 collective-permute-start.7
  1.1 2.6 %collective-permute-start.12 = (bf16[128,6144]{1,0:T(8,128)(2,1)}, bf16[128,6144]{1,0:T(8,128)(2,1)S(1)}, u32[]{:S(2)}, u32[]{:S(2)}) collective-permute-start(bf16[128,6144]{1,0:T(8,128)(2,1)} %refs_0_.5), channel_id=1, source_target_pairs={{2,0},{0,2},{3,1},{1,3},{6,4},{4,6},{7,5},{5,7},{10,8},{8,10},{11,... | collective-permute-start | bytes 4718600 | tf_op jit(solution)/shard_map/ppermute | solution.py:42
  3.7 0.0 copy-start.1
  3.7 1.0 %copy-done.1 = bf16[128,1536]{1,0:T(8,128)(2,1)S(1)} copy-done((bf16[128,1536]{1,0:T(8,128)(2,1)S(1)}, bf16[128,1536]{1,0:T(8,128)(2,1)}, u32[]{:S(2)}) %copy-start.1) | copy-done | bytes 393240
  4.7 1.6 %collective-permute-start.3 = (bf16[64,1536]{1,0:T(8,128)(2,1)S(1)}, bf16[64,1536]{1,0:T(8,128)(2,1)S(1)}, u32[]{:S(2)}, u32[]{:S(2)}) collective-permute-start(bf16[64,1536]{1,0:T(8,128)(2,1)S(1)} %get-tuple-element.16.refs_4_), channel_id=1, source_target_pairs={{0,4},{4,8},{8,12},{12,0},{1,5},{5,9},{9,13},{13,1},{2,6},{6,10},{... | collective-permute-start | bytes 589832 | tf_op jit(solution)/shard_map/ppermute | solution.py:38
  6.4 1.6 %collective-permute-start = (bf16[64,1536]{1,0:T(8,128)(2,1)S(1)}, bf16[64,1536]{1,0:T(8,128)(2,1)S(1)}, u32[]{:S(2)}, u32[]{:S(2)}) collective-permute-start(bf16[64,1536]{1,0:T(8,128)(2,1)S(1)} %get-tuple-element.15.refs_1_.refs_0_), channel_id=1, source_target_pairs={{0,4},{4,8},{8,12},{12,0},{1,5},{5,9},{9,13},{13,1},{2,6},{6,10},{... | collective-permute-start | bytes 589832 | tf_op jit(solution)/shard_map/ppermute | solution.py:38
  7.9 6.4 %collective-permute-done.3.refs_5_ = bf16[64,1536]{1,0:T(8,128)(2,1)S(1)} collective-permute-done((bf16[64,1536]{1,0:T(8,128)(2,1)S(1)}, bf16[64,1536]{1,0:T(8,128)(2,1)S(1)}, u32[]{:S(2)}, u32[]{:S(2)}) %collective-permute-start.3) | collective-permute-done | bytes 196640 | tf_op jit(solution)/shard_map/ppermute | solution.py:38
  14.3 0.0 collective-permute-start.4
  14.3 3.9 %collective-permute-done.refs_1_ = bf16[64,1536]{1,0:T(8,128)(2,1)S(1)} collective-permute-done((bf16[64,1536]{1,0:T(8,128)(2,1)S(1)}, bf16[64,1536]{1,0:T(8,128)(2,1)S(1)}, u32[]{:S(2)}, u32[]{:S(2)}) %collective-permute-start) | collective-permute-done | bytes 196640 | tf_op jit(solution)/shard_map/ppermute | solution.py:38
  18.2 0.1 collective-permute-start.1
  18.3 4.1 %collective-permute-done.4.refs_6_ = bf16[64,1536]{1,0:T(8,128)(2,1)S(1)} collective-permute-done((bf16[64,1536]{1,0:T(8,128)(2,1)S(1)}, bf16[64,1536]{1,0:T(8,128)(2,1)S(1)}, u32[]{:S(2)}, u32[]{:S(2)}) %collective-permute-start.4) | collective-permute-done | bytes 196640 | tf_op jit(solution)/shard_map/ppermute | solution.py:38
  22.4 0.1 collective-permute-start.5
  22.5 5.3 %collective-permute-done.1.refs_2_ = bf16[64,1536]{1,0:T(8,128)(2,1)S(1)} collective-permute-done((bf16[64,1536]{1,0:T(8,128)(2,1)S(1)}, bf16[64,1536]{1,0:T(8,128)(2,1)S(1)}, u32[]{:S(2)}, u32[]{:S(2)}) %collective-permute-start.1) | collective-permute-done | bytes 196640 | tf_op jit(solution)/shard_map/ppermute | solution.py:38
  27.8 0.0 collective-permute-start.2
  27.8 0.0 copy-start
  27.8 1.4 %copy-done = bf16[128,6144]{1,0:T(8,128)(2,1)S(1)} copy-done((bf16[128,6144]{1,0:T(8,128)(2,1)S(1)}, bf16[128,6144]{1,0:T(8,128)(2,1)}, u32[]{:S(2)}) %copy-start) | copy-done | bytes 1572888
  29.2 1.4 %hidden_part.1.refs_1_.refs_0_ = bf16[128,6144]{1,0:T(8,128)(2,1)S(1)} custom-call(bf16[128,6144]{1,0:T(8,128)(2,1)S(1)} %copy-done, bf16[64,1536]{1,0:T(8,128)(2,1)S(1)} %get-tuple-element.15.refs_1_.refs_0_), custom_call_target="tpu_custom_call" | custom-call | bytes 1024 | tf_op jit(solution)/shard_map/hidden_part/pallas_call | solution.py:72
  30.7 2.4 %slopes.1.refs_8_.refs_0_ = f32[128,6144]{1,0:T(8,128)S(1)} custom-call(bf16[128,6144]{1,0:T(8,128)(2,1)S(1)} %copy-done, bf16[128,6144]{1,0:T(8,128)(2,1)S(1)} %hidden_part.1.refs_1_.refs_0_), custom_call_target="tpu_custom_call" | custom-call | bytes 1024 | tf_op jit(solution)/shard_map/slopes/pallas_call | solution.py:72
  33.0 0.0 collective-permute-done.5.refs_7_
  33.1 2.2 %collective-permute-done.2.refs_3_ = bf16[64,1536]{1,0:T(8,128)(2,1)S(1)} collective-permute-done((bf16[64,1536]{1,0:T(8,128)(2,1)S(1)}, bf16[64,1536]{1,0:T(8,128)(2,1)S(1)}, u32[]{:S(2)}, u32[]{:S(2)}) %collective-permute-start.2) | collective-permute-done | bytes 196640 | tf_op jit(solution)/shard_map/ppermute | solution.py:38
  35.3 0.2 in_order.1
  35.5 0.1 collective-permute-start.6
  35.6 0.5 collective-permute-start.13
  36.1 1.8 %collective-permute-done.6.refs_1_ = bf16[256,1536]{1,0:T(8,128)(2,1)S(1)} collective-permute-done((bf16[256,1536]{1,0:T(8,128)(2,1)S(1)}, bf16[256,1536]{1,0:T(8,128)(2,1)S(1)}, u32[]{:S(2)}, u32[]{:S(2)}) %collective-permute-start.6) | collective-permute-done | bytes 786464 | tf_op jit(solution)/shard_map/ppermute | solution.py:38
  37.9 0.0 collective-permute-done.7.refs_3_
  37.9 5.3 %partial_products.4 = (f32[128,1536]{1,0:T(8,128)S(1)}, bf16[128,1536]{1,0:T(8,128)(2,1)S(1)}) custom-call(bf16[256,1536]{1,0:T(8,128)(2,1)S(1)} %get-tuple-element.17.refs_0_.refs_4_, bf16[256,1536]{1,0:T(8,128)(2,1)S(1)} %collective-permute-done.6.refs_1_, bf16[6144,1536]{1,0:T(8,128)(2,1)} %refs_2_.7, bf16[6144,1536]{1,0:T(8,128)(2,1)} %collective-permute-done.7.refs_3_), custom_call_target="tpu_custom_call" | custom-call | flops 24159192 | bytes 1024 | tf_op jit(solution)/shard_map/partial_products/pallas_call | solution.py:72
  43.1 0.0 collective-permute-done.12.refs_1_
  43.2 0.2 collective-permute-start.14
  43.4 0.3 collective-permute-start.11
  43.7 5.3 %partial_products.5 = (f32[128,1536]{1,0:T(8,128)S(1)}, bf16[128,1536]{1,0:T(8,128)(2,1)S(1)}) custom-call(bf16[256,1536]{1,0:T(8,128)(2,1)S(1)} %get-tuple-element.17.refs_0_.refs_4_, bf16[256,1536]{1,0:T(8,128)(2,1)S(1)} %collective-permute-done.6.refs_1_, bf16[6144,1536]{1,0:T(8,128)(2,1)} %refs_2_.7, bf16[6144,1536]{1,0:T(8,128)(2,1)} %collective-permute-done.7.refs_3_, ...), custom_call_target="tpu_custom_call" | custom-call | flops 24159192 | bytes 1024 | tf_op jit(solution)/shard_map/partial_products/pallas_call | solution.py:72
  49.0 1.8 %collective-permute-start.10 = (bf16[128,1536]{1,0:T(8,128)(2,1)S(1)}, bf16[128,1536]{1,0:T(8,128)(2,1)S(1)}, u32[]{:S(2)}, u32[]{:S(2)}) collective-permute-start(bf16[128,1536]{1,0:T(8,128)(2,1)S(1)} %get-tuple-element.25), channel_id=1, source_target_pairs={{0,2},{2,0},{1,3},{3,1},{4,6},{6,4},{5,7},{7,5},{8,10},{10,8},{9,1... | collective-permute-start | bytes 1179656 | tf_op jit(solution)/shard_map/ppermute | solution.py:38
  50.8 5.3 %partial_products.6 = (f32[128,1536]{1,0:T(8,128)S(1)}, bf16[128,1536]{1,0:T(8,128)(2,1)S(1)}) custom-call(bf16[256,1536]{1,0:T(8,128)(2,1)S(1)} %get-tuple-element.17.refs_0_.refs_4_, bf16[256,1536]{1,0:T(8,128)(2,1)S(1)} %collective-permute-done.6.refs_1_, bf16[6144,1536]{1,0:T(8,128)(2,1)} %refs_2_.7, bf16[6144,1536]{1,0:T(8,128)(2,1)} %collective-permute-done.7.refs_3_, ...), custom_call_target="tpu_custom_call" | custom-call | flops 24159192 | bytes 1024 | tf_op jit(solution)/shard_map/partial_products/pallas_call | solution.py:72
  56.1 0.3 collective-permute-start.9
  56.4 5.3 %partial_products.7 = (f32[128,1536]{1,0:T(8,128)S(1)}, bf16[128,1536]{1,0:T(8,128)(2,1)S(1)}) custom-call(bf16[256,1536]{1,0:T(8,128)(2,1)S(1)} %get-tuple-element.17.refs_0_.refs_4_, bf16[256,1536]{1,0:T(8,128)(2,1)S(1)} %collective-permute-done.6.refs_1_, bf16[6144,1536]{1,0:T(8,128)(2,1)} %refs_2_.7, bf16[6144,1536]{1,0:T(8,128)(2,1)} %collective-permute-done.7.refs_3_, ...), custom_call_target="tpu_custom_call" | custom-call | flops 24159192 | bytes 1024 | tf_op jit(solution)/shard_map/partial_products/pallas_call | solution.py:72
  61.7 0.0 collective-permute-done.13.refs_2_
  61.7 1.8 %collective-permute-start.8 = (bf16[128,1536]{1,0:T(8,128)(2,1)S(1)}, bf16[128,1536]{1,0:T(8,128)(2,1)S(1)}, u32[]{:S(2)}, u32[]{:S(2)}) collective-permute-start(bf16[128,1536]{1,0:T(8,128)(2,1)S(1)} %get-tuple-element.23), channel_id=1, source_target_pairs={{0,2},{2,0},{1,3},{3,1},{4,6},{6,4},{5,7},{7,5},{8,10},{10,8},{9,1... | collective-permute-start | bytes 1179656 | tf_op jit(solution)/shard_map/ppermute | solution.py:38
  63.6 0.0 collective-permute-done.14.refs_3_
  63.6 13.5 %weight_products.1.refs_3_ = bf16[6144,1536]{1,0:T(8,128)(2,1)} custom-call(bf16[128,6144]{1,0:T(8,128)(2,1)S(1)} %hidden_part.1.refs_1_.refs_0_, bf16[128,6144]{1,0:T(8,128)(2,1)S(1)} %collective-permute-done.12.refs_1_, bf16[128,6144]{1,0:T(8,128)(2,1)S(1)} %collective-permute-done.13.refs_2_, bf16[128,6144]{1,0:T(8,128)(2,1)S(1)} %collective-permute-done.14.refs_3_, ...), custom_call_target="tpu_custom_call" | custom-call | flops 1024 | bytes 1024 | tf_op jit(solution)/shard_map/weight_products/pallas_call | solution.py:72
  77.1 0.0 collective-permute-done.11.refs_2_
  77.1 0.8 %last_step.4.refs_3_ = bf16[128,6144]{1,0:T(8,128)(2,1)} custom-call(f32[128,6144]{1,0:T(8,128)S(1)} %slopes.1.refs_8_.refs_0_, f32[128,1536]{1,0:T(8,128)S(1)} %get-tuple-element.19.refs_4_.refs_1_, bf16[128,1536]{1,0:T(8,128)(2,1)S(1)} %collective-permute-done.11.refs_2_, bf16[6144,1536]{1,0:T(8,128)(2,1)} %weight_products.1.refs_3_), custom_call_target="tpu_custom_call" | custom-call | flops 161061280 | bytes 1024 | tf_op jit(solution)/shard_map/last_step/pallas_call | solution.py:72
  77.9 0.0 collective-permute-done.10.refs_2_
  77.9 0.8 %last_step.5.refs_3_ = bf16[128,6144]{1,0:T(8,128)(2,1)} custom-call(f32[128,6144]{1,0:T(8,128)S(1)} %slopes.1.refs_8_.refs_0_, f32[128,1536]{1,0:T(8,128)S(1)} %get-tuple-element.20.refs_4_.refs_1_, bf16[128,1536]{1,0:T(8,128)(2,1)S(1)} %collective-permute-done.10.refs_2_, bf16[128,6144]{1,0:T(8,128)(2,1)} %last_step.4.refs_3_), custom_call_target="tpu_custom_call", output_to_operand_aliasing={{}: (3, {})} | custom-call | flops 161061280 | bytes 1024 | tf_op jit(solution)/shard_map/last_step/pallas_call | solution.py:72
  78.8 0.0 collective-permute-done.9.refs_2_
  78.8 0.8 %last_step.6.refs_3_ = bf16[128,6144]{1,0:T(8,128)(2,1)} custom-call(f32[128,6144]{1,0:T(8,128)S(1)} %slopes.1.refs_8_.refs_0_, f32[128,1536]{1,0:T(8,128)S(1)} %get-tuple-element.21.refs_4_.refs_1_, bf16[128,1536]{1,0:T(8,128)(2,1)S(1)} %collective-permute-done.9.refs_2_, bf16[128,6144]{1,0:T(8,128)(2,1)} %last_step.5.refs_3_), custom_call_target="tpu_custom_call", output_to_operand_aliasing={{}: (3, {})} | custom-call | flops 161061280 | bytes 1024 | tf_op jit(solution)/shard_map/last_step/pallas_call | solution.py:72
  79.6 0.4 collective-permute-done.8.refs_2_
  80.0 0.8 %last_step.7 = bf16[128,6144]{1,0:T(8,128)(2,1)} custom-call(f32[128,6144]{1,0:T(8,128)S(1)} %slopes.1.refs_8_.refs_0_, f32[128,1536]{1,0:T(8,128)S(1)} %get-tuple-element.22.refs_6_.refs_1_, bf16[128,1536]{1,0:T(8,128)(2,1)S(1)} %collective-permute-done.8.refs_2_, bf16[128,6144]{1,0:T(8,128)(2,1)} %last_step.6.refs_3_), custom_call_target="tpu_custom_call", output_to_operand_aliasing={{}: (3, {})} | custom-call | flops 161061280 | bytes 1024 | tf_op jit(solution)/shard_map/last_step/pallas_call | solution.py:72
  (1 shorter events, 0.0 us)
Async XLA Ops:
  0.6 37.2 %collective-permute-start.7 = (bf16[6144,1536]{1,0:T(8,128)(2,1)}, bf16[6144,1536]{1,0:T(8,128)(2,1)}, u32[]{:S(2)}, u32[]{:S(2)}) collective-permute-start(bf16[6144,1536]{1,0:T(8,128)(2,1)} %refs_2_.7), channel_id=1, source_target_pairs={{1,0},{0,1},{3,2},{2,3},{5,4},{4,5},{7,6},{6,7},{9,8},{8,9},{11,10... | collective-permute-start | bytes 56623112 | tf_op jit(solution)/shard_map/ppermute | solution.py:42
  1.1 42.0 %collective-permute-start.12 = (bf16[128,6144]{1,0:T(8,128)(2,1)}, bf16[128,6144]{1,0:T(8,128)(2,1)S(1)}, u32[]{:S(2)}, u32[]{:S(2)}) collective-permute-start(bf16[128,6144]{1,0:T(8,128)(2,1)} %refs_0_.5), channel_id=1, source_target_pairs={{2,0},{0,2},{3,1},{1,3},{6,4},{4,6},{7,5},{5,7},{10,8},{8,10},{11,... | collective-permute-start | bytes 4718600 | tf_op jit(solution)/shard_map/ppermute | solution.py:42
  3.7 1.0 %copy-start.1 = (bf16[128,1536]{1,0:T(8,128)(2,1)S(1)}, bf16[128,1536]{1,0:T(8,128)(2,1)}, u32[]{:S(2)}) copy-start(bf16[128,1536]{1,0:T(8,128)(2,1)} %refs_0_.3) | copy-start | bytes 1179652
  4.7 9.6 %collective-permute-start.3 = (bf16[64,1536]{1,0:T(8,128)(2,1)S(1)}, bf16[64,1536]{1,0:T(8,128)(2,1)S(1)}, u32[]{:S(2)}, u32[]{:S(2)}) collective-permute-start(bf16[64,1536]{1,0:T(8,128)(2,1)S(1)} %get-tuple-element.16.refs_4_), channel_id=1, source_target_pairs={{0,4},{4,8},{8,12},{12,0},{1,5},{5,9},{9,13},{13,1},{2,6},{6,10},{... | collective-permute-start | bytes 589832 | tf_op jit(solution)/shard_map/ppermute | solution.py:38
  6.4 11.8 %collective-permute-start = (bf16[64,1536]{1,0:T(8,128)(2,1)S(1)}, bf16[64,1536]{1,0:T(8,128)(2,1)S(1)}, u32[]{:S(2)}, u32[]{:S(2)}) collective-permute-start(bf16[64,1536]{1,0:T(8,128)(2,1)S(1)} %get-tuple-element.15.refs_1_.refs_0_), channel_id=1, source_target_pairs={{0,4},{4,8},{8,12},{12,0},{1,5},{5,9},{9,13},{13,1},{2,6},{6,10},{... | collective-permute-start | bytes 589832 | tf_op jit(solution)/shard_map/ppermute | solution.py:38
  14.3 8.1 %collective-permute-start.4 = (bf16[64,1536]{1,0:T(8,128)(2,1)S(1)}, bf16[64,1536]{1,0:T(8,128)(2,1)S(1)}, u32[]{:S(2)}, u32[]{:S(2)}) collective-permute-start(bf16[64,1536]{1,0:T(8,128)(2,1)S(1)} %collective-permute-done.3.refs_5_), channel_id=1, source_target_pairs={{0,4},{4,8},{8,12},{12,0},{1,5},{5,9},{9,13},{13,1},{2,6},{6,10},{... | collective-permute-start | bytes 589832 | tf_op jit(solution)/shard_map/ppermute | solution.py:38
  18.2 9.6 %collective-permute-start.1 = (bf16[64,1536]{1,0:T(8,128)(2,1)S(1)}, bf16[64,1536]{1,0:T(8,128)(2,1)S(1)}, u32[]{:S(2)}, u32[]{:S(2)}) collective-permute-start(bf16[64,1536]{1,0:T(8,128)(2,1)S(1)} %collective-permute-done.refs_1_), channel_id=1, source_target_pairs={{0,4},{4,8},{8,12},{12,0},{1,5},{5,9},{9,13},{13,1},{2,6},{6,10},{... | collective-permute-start | bytes 589832 | tf_op jit(solution)/shard_map/ppermute | solution.py:38
  22.4 10.6 %collective-permute-start.5 = (bf16[64,1536]{1,0:T(8,128)(2,1)S(1)}, bf16[64,1536]{1,0:T(8,128)(2,1)S(1)}, u32[]{:S(2)}, u32[]{:S(2)}) collective-permute-start(bf16[64,1536]{1,0:T(8,128)(2,1)S(1)} %collective-permute-done.4.refs_6_), channel_id=1, source_target_pairs={{0,4},{4,8},{8,12},{12,0},{1,5},{5,9},{9,13},{13,1},{2,6},{6,10},{... | collective-permute-start | bytes 589832 | tf_op jit(solution)/shard_map/ppermute | solution.py:38
  27.8 7.5 %collective-permute-start.2 = (bf16[64,1536]{1,0:T(8,128)(2,1)S(1)}, bf16[64,1536]{1,0:T(8,128)(2,1)S(1)}, u32[]{:S(2)}, u32[]{:S(2)}) collective-permute-start(bf16[64,1536]{1,0:T(8,128)(2,1)S(1)} %collective-permute-done.1.refs_2_), channel_id=1, source_target_pairs={{0,4},{4,8},{8,12},{12,0},{1,5},{5,9},{9,13},{13,1},{2,6},{6,10},{... | collective-permute-start | bytes 589832 | tf_op jit(solution)/shard_map/ppermute | solution.py:38
  27.8 1.4 %copy-start = (bf16[128,6144]{1,0:T(8,128)(2,1)S(1)}, bf16[128,6144]{1,0:T(8,128)(2,1)}, u32[]{:S(2)}) copy-start(bf16[128,6144]{1,0:T(8,128)(2,1)} %refs_0_.5) | copy-start | bytes 4718596
  35.5 2.4 %collective-permute-start.6 = (bf16[256,1536]{1,0:T(8,128)(2,1)S(1)}, bf16[256,1536]{1,0:T(8,128)(2,1)S(1)}, u32[]{:S(2)}, u32[]{:S(2)}) collective-permute-start(bf16[256,1536]{1,0:T(8,128)(2,1)S(1)} %get-tuple-element.18.refs_5_), channel_id=1, source_target_pairs={{0,1},{1,0},{2,3},{3,2},{4,5},{5,4},{6,7},{7,6},{8,9},{9,8},{10,11... | collective-permute-start | bytes 2359304 | tf_op jit(solution)/shard_map/ppermute | solution.py:38
  35.6 26.2 %collective-permute-start.13 = (bf16[128,6144]{1,0:T(8,128)(2,1)S(1)}, bf16[128,6144]{1,0:T(8,128)(2,1)S(1)}, u32[]{:S(2)}, u32[]{:S(2)}) collective-permute-start(bf16[128,6144]{1,0:T(8,128)(2,1)S(1)} %hidden_part.1.refs_1_.refs_0_), channel_id=1, source_target_pairs={{1,0},{0,1},{3,2},{2,3},{5,4},{4,5},{7,6},{6,7},{9,8},{8,9},{11,10... | collective-permute-start | bytes 4718600 | tf_op jit(solution)/shard_map/ppermute | solution.py:42
  43.2 20.4 %collective-permute-start.14 = (bf16[128,6144]{1,0:T(8,128)(2,1)S(1)}, bf16[128,6144]{1,0:T(8,128)(2,1)S(1)}, u32[]{:S(2)}, u32[]{:S(2)}) collective-permute-start(bf16[128,6144]{1,0:T(8,128)(2,1)S(1)} %collective-permute-done.12.refs_1_), channel_id=1, source_target_pairs={{1,0},{0,1},{3,2},{2,3},{5,4},{4,5},{7,6},{6,7},{9,8},{8,9},{11,10... | collective-permute-start | bytes 4718600 | tf_op jit(solution)/shard_map/ppermute | solution.py:42
  43.4 33.7 %collective-permute-start.11 = (bf16[128,1536]{1,0:T(8,128)(2,1)S(1)}, bf16[128,1536]{1,0:T(8,128)(2,1)S(1)}, u32[]{:S(2)}, u32[]{:S(2)}) collective-permute-start(bf16[128,1536]{1,0:T(8,128)(2,1)S(1)} %get-tuple-element.26), channel_id=1, source_target_pairs={{0,2},{2,0},{1,3},{3,1},{4,6},{6,4},{5,7},{7,5},{8,10},{10,8},{9,1... | collective-permute-start | bytes 1179656 | tf_op jit(solution)/shard_map/ppermute | solution.py:38
  49.0 29.0 %collective-permute-start.10 = (bf16[128,1536]{1,0:T(8,128)(2,1)S(1)}, bf16[128,1536]{1,0:T(8,128)(2,1)S(1)}, u32[]{:S(2)}, u32[]{:S(2)}) collective-permute-start(bf16[128,1536]{1,0:T(8,128)(2,1)S(1)} %get-tuple-element.25), channel_id=1, source_target_pairs={{0,2},{2,0},{1,3},{3,1},{4,6},{6,4},{5,7},{7,5},{8,10},{10,8},{9,1... | collective-permute-start | bytes 1179656 | tf_op jit(solution)/shard_map/ppermute | solution.py:38
  56.1 22.7 %collective-permute-start.9 = (bf16[128,1536]{1,0:T(8,128)(2,1)S(1)}, bf16[128,1536]{1,0:T(8,128)(2,1)S(1)}, u32[]{:S(2)}, u32[]{:S(2)}) collective-permute-start(bf16[128,1536]{1,0:T(8,128)(2,1)S(1)} %get-tuple-element.24), channel_id=1, source_target_pairs={{0,2},{2,0},{1,3},{3,1},{4,6},{6,4},{5,7},{7,5},{8,10},{10,8},{9,1... | collective-permute-start | bytes 1179656 | tf_op jit(solution)/shard_map/ppermute | solution.py:38
  61.7 18.3 %collective-permute-start.8 = (bf16[128,1536]{1,0:T(8,128)(2,1)S(1)}, bf16[128,1536]{1,0:T(8,128)(2,1)S(1)}, u32[]{:S(2)}, u32[]{:S(2)}) collective-permute-start(bf16[128,1536]{1,0:T(8,128)(2,1)S(1)} %get-tuple-element.23), channel_id=1, source_target_pairs={{0,2},{2,0},{1,3},{3,1},{4,6},{6,4},{5,7},{7,5},{8,10},{10,8},{9,1... | collective-permute-start | bytes 1179656 | tf_op jit(solution)/shard_map/ppermute | solution.py:38

commit v5 on v4

--- a/solution.py
+++ b/solution.py
@@ -184,7 +184,27 @@
     )
 
 
-def partial_products(grads, weights, offset, size, block, after):
+def staged(weight, size, after):
+    width = weight.shape[1]
+    tile = tile_of(0, size)
+
+    def kernel(weight_ref, copy_ref):
+        copy_ref[...] = weight_ref[...]
+
+    spec = pl.BlockSpec((tile, width), lambda i: (i, 0))
+    return call(
+        kernel,
+        "staged",
+        (size // tile,),
+        [weight],
+        [spec],
+        [jax.ShapeDtypeStruct((size, width), bf16)],
+        [spec],
+        after,
+    )[0]
+
+
+def partial_products(grads, weights, offset, size, block, after, held=None):
     half, width = grads[0].shape
     tile = tile_of(offset, size)
     start = offset // tile
@@ -193,20 +213,24 @@
     def kernel(*refs):
         own_ref, send_ref = refs[-2:]
         product = 0.0
-        for part, rows in zip(refs[:count], refs[count:-2]):
+        here = pl.ds(pl.multiple_of(pl.program_id(0) * tile, tile), tile)
+        for k, (part, rows) in enumerate(zip(refs[:count], refs[count:-2])):
+            rows_of = rows[here] if k == 0 and held is not None else rows[...]
             product = product + lax.dot_general(
-                part[...], rows[...], (((1,), (1,)), ((), ())), preferred_element_type=f32
+                part[...], rows_of, (((1,), (1,)), ((), ())), preferred_element_type=f32
             )
         own_ref[...] = product[:block]
         send_ref[...] = product[block:].astype(bf16)
 
+    spec = pl.BlockSpec((tile, width), lambda i: (start + i, 0))
     return call(
         kernel,
         "partial_products",
         (size // tile,),
-        [*grads, *weights],
+        [*grads, *(weights if held is None else [held, *weights[1:]])],
         [fixed((half, width))] * count
-        + [pl.BlockSpec((tile, width), lambda i: (start + i, 0))] * count,
+        + [spec if held is None else fixed((size, width))]
+        + [spec] * (count - 1),
         [
             jax.ShapeDtypeStruct((block, size), f32),
             jax.ShapeDtypeStruct((half - block, size), bf16),
@@ -317,7 +341,8 @@
             return (dd * cols + dx) * per_block + lax.rem(row, per_block)
 
         hops = range(1, depths)
-        first, second = in_order(pieces, place_of, half, tokens, [slope])
+        early = staged(weight, cut(features, PARTIAL_CUTS)[0][1], [slope])
+        first, second = in_order(pieces, place_of, half, tokens, [early])
         weights = [weight] + [from_next(weight, "depth", depths, dd) for dd in hops]
         grads = [first] + [
             to_next(second[(dd - 1) * half : dd * half], "depth", depths, dd) for dd in hops
@@ -328,7 +353,10 @@
         owns, far = [], []
         for c, (offset, size) in enumerate(chunks):
             after = owns[-1:]
-            own, send = partial_products(grads, weights, offset, size, block, after)
+            own, send = partial_products(
+                grads, weights, offset, size, block, after,
+                early if c == 0 else None,
+            )
             owns.append(own)
             far.append(
                 [

time: 81.1 us -> 80.7 us (level)
  waiting for transfers between devices: 24 us -> 21.8 us
  Pallas kernels: 42.1 us -> 44 us
    ppermute x11, waiting for transfers between devices: 24 us -> 21.8 us  [to_next(): lax.ppermute(array, axis, [(i, (i + hop) % size) for i in range(size)])]
    pallas_call x13 -> x14, Pallas kernels: 42.1 us -> 44 us  [call(): pl.pallas_call(body, grid=grid, in_specs=list(in_specs) + [ANY] * len(ext...]
  transfers between devices with their start and end apart: 15 -> 15, of which waited for: 7 -> 6; matrix products, arithmetic and copies ran while one was open for 0% -> 0% of each run, Pallas kernels for 51% -> 54%
where the time goes in v5:
time: 80.7 us; the launch traced here: 80.5 us
  Pallas kernels  44 us (55%)
  waiting for transfers between devices  21.8 us (27%)
  starting transfers between devices  11.6 us (14%)
  local copies, waits for them, and re-layouts  2.4 us (3%)
    pallas_call x14, Pallas kernels, call(): pl.pallas_call(body, grid=grid, in_specs=list(in_specs) + [ANY] * len(ext...  44 us
    ppermute x11, waiting for transfers between devices, to_next(): lax.ppermute(array, axis, [(i, (i + hop) % size) for i in range(size)])  21.8 us
    ppermute x11, starting transfers between devices, to_next(): lax.ppermute(array, axis, [(i, (i + hop) % size) for i in range(size)])  7.85 us
    ppermute x4, starting transfers between devices, from_next(): lax.ppermute(array, axis, [((i + hop) % size, i) for i in range(size)])  3.78 us
    unnamed x4, local copies, waits for them, and re-layouts  2.4 us
  transfers between devices with their start and end apart: 15, of which 6 were waited for; matrix products, arithmetic and copies ran while one was open for 0% of the time, Pallas kernels for 54%

profile of v5, /device:TPU:0, one launch (start us, length us, event | category | flops | bytes accessed | tf_op | source)
XLA Modules:
  0.0 80.5 jit_solution(9504356284160735640)
XLA Ops:
  0.6 0.5 collective-permute-start.7
  1.1 2.6 %collective-permute-start.12 = (bf16[128,6144]{1,0:T(8,128)(2,1)}, bf16[128,6144]{1,0:T(8,128)(2,1)S(1)}, u32[]{:S(2)}, u32[]{:S(2)}) collective-permute-start(bf16[128,6144]{1,0:T(8,128)(2,1)} %refs_0_.6), channel_id=1, source_target_pairs={{2,0},{0,2},{3,1},{1,3},{6,4},{4,6},{7,5},{5,7},{10,8},{8,10},{11,... | collective-permute-start | bytes 4718600 | tf_op jit(solution)/shard_map/ppermute | solution.py:42
  3.7 0.0 copy-start.1
  3.7 1.0 %copy-done.1 = bf16[128,1536]{1,0:T(8,128)(2,1)S(1)} copy-done((bf16[128,1536]{1,0:T(8,128)(2,1)S(1)}, bf16[128,1536]{1,0:T(8,128)(2,1)}, u32[]{:S(2)}) %copy-start.1) | copy-done | bytes 393240
  4.7 1.6 %collective-permute-start = (bf16[64,1536]{1,0:T(8,128)(2,1)S(1)}, bf16[64,1536]{1,0:T(8,128)(2,1)S(1)}, u32[]{:S(2)}, u32[]{:S(2)}) collective-permute-start(bf16[64,1536]{1,0:T(8,128)(2,1)S(1)} %get-tuple-element.15.refs_1_.refs_0_), channel_id=1, source_target_pairs={{0,4},{4,8},{8,12},{12,0},{1,5},{5,9},{9,13},{13,1},{2,6},{6,10},{... | collective-permute-start | bytes 589832 | tf_op jit(solution)/shard_map/ppermute | solution.py:38
  6.4 1.6 %collective-permute-start.3 = (bf16[64,1536]{1,0:T(8,128)(2,1)S(1)}, bf16[64,1536]{1,0:T(8,128)(2,1)S(1)}, u32[]{:S(2)}, u32[]{:S(2)}) collective-permute-start(bf16[64,1536]{1,0:T(8,128)(2,1)S(1)} %get-tuple-element.16.refs_4_), channel_id=1, source_target_pairs={{0,4},{4,8},{8,12},{12,0},{1,5},{5,9},{9,13},{13,1},{2,6},{6,10},{... | collective-permute-start | bytes 589832 | tf_op jit(solution)/shard_map/ppermute | solution.py:38
  7.9 6.4 %collective-permute-done.refs_1_ = bf16[64,1536]{1,0:T(8,128)(2,1)S(1)} collective-permute-done((bf16[64,1536]{1,0:T(8,128)(2,1)S(1)}, bf16[64,1536]{1,0:T(8,128)(2,1)S(1)}, u32[]{:S(2)}, u32[]{:S(2)}) %collective-permute-start) | collective-permute-done | bytes 196640 | tf_op jit(solution)/shard_map/ppermute | solution.py:38
  14.3 0.0 collective-permute-start.1
  14.3 3.9 %collective-permute-done.3.refs_5_ = bf16[64,1536]{1,0:T(8,128)(2,1)S(1)} collective-permute-done((bf16[64,1536]{1,0:T(8,128)(2,1)S(1)}, bf16[64,1536]{1,0:T(8,128)(2,1)S(1)}, u32[]{:S(2)}, u32[]{:S(2)}) %collective-permute-start.3) | collective-permute-done | bytes 196640 | tf_op jit(solution)/shard_map/ppermute | solution.py:38
  18.2 0.1 collective-permute-start.4
  18.3 4.1 %collective-permute-done.1.refs_2_ = bf16[64,1536]{1,0:T(8,128)(2,1)S(1)} collective-permute-done((bf16[64,1536]{1,0:T(8,128)(2,1)S(1)}, bf16[64,1536]{1,0:T(8,128)(2,1)S(1)}, u32[]{:S(2)}, u32[]{:S(2)}) %collective-permute-start.1) | collective-permute-done | bytes 196640 | tf_op jit(solution)/shard_map/ppermute | solution.py:38
  22.4 0.1 collective-permute-start.2
  22.5 5.3 %collective-permute-done.4.refs_6_ = bf16[64,1536]{1,0:T(8,128)(2,1)S(1)} collective-permute-done((bf16[64,1536]{1,0:T(8,128)(2,1)S(1)}, bf16[64,1536]{1,0:T(8,128)(2,1)S(1)}, u32[]{:S(2)}, u32[]{:S(2)}) %collective-permute-start.4) | collective-permute-done | bytes 196640 | tf_op jit(solution)/shard_map/ppermute | solution.py:38
  27.8 0.0 collective-permute-start.5
  27.8 0.0 copy-start
  27.8 1.4 %copy-done = bf16[128,6144]{1,0:T(8,128)(2,1)S(1)} copy-done((bf16[128,6144]{1,0:T(8,128)(2,1)S(1)}, bf16[128,6144]{1,0:T(8,128)(2,1)}, u32[]{:S(2)}) %copy-start) | copy-done | bytes 1572888
  29.2 1.4 %hidden_part.1.refs_1_.refs_0_ = bf16[128,6144]{1,0:T(8,128)(2,1)S(1)} custom-call(bf16[128,6144]{1,0:T(8,128)(2,1)S(1)} %copy-done, bf16[64,1536]{1,0:T(8,128)(2,1)S(1)} %get-tuple-element.15.refs_1_.refs_0_), custom_call_target="tpu_custom_call" | custom-call | bytes 1024 | tf_op jit(solution)/shard_map/hidden_part/pallas_call | solution.py:72
  30.7 2.4 %slopes.1.refs_1_.refs_0_ = f32[128,6144]{1,0:T(8,128)S(1)} custom-call(bf16[128,6144]{1,0:T(8,128)(2,1)S(1)} %copy-done, bf16[128,6144]{1,0:T(8,128)(2,1)S(1)} %hidden_part.1.refs_1_.refs_0_), custom_call_target="tpu_custom_call" | custom-call | bytes 1024 | tf_op jit(solution)/shard_map/slopes/pallas_call | solution.py:72
  33.0 2.6 %staged.1.refs_8_.refs_2_ = bf16[1536,1536]{1,0:T(8,128)(2,1)S(1)} custom-call(bf16[6144,1536]{1,0:T(8,128)(2,1)} %refs_2_.5, f32[128,6144]{1,0:T(8,128)S(1)} %slopes.1.refs_1_.refs_0_), custom_call_target="tpu_custom_call" | custom-call | bytes 1024 | tf_op jit(solution)/shard_map/staged/pallas_call | solution.py:72
  35.6 0.0 collective-permute-done.2.refs_3_
  35.6 0.0 collective-permute-done.5.refs_7_
  35.6 0.2 in_order.1
  35.9 0.1 collective-permute-start.6
  36.0 0.5 collective-permute-start.13
  36.4 1.8 %collective-permute-done.6.refs_1_ = bf16[256,1536]{1,0:T(8,128)(2,1)S(1)} collective-permute-done((bf16[256,1536]{1,0:T(8,128)(2,1)S(1)}, bf16[256,1536]{1,0:T(8,128)(2,1)S(1)}, u32[]{:S(2)}, u32[]{:S(2)}) %collective-permute-start.6) | collective-permute-done | bytes 786464 | tf_op jit(solution)/shard_map/ppermute | solution.py:38
  38.2 0.0 collective-permute-done.7.refs_3_
  38.2 4.6 %partial_products.4 = (f32[128,1536]{1,0:T(8,128)S(1)}, bf16[128,1536]{1,0:T(8,128)(2,1)S(1)}) custom-call(bf16[256,1536]{1,0:T(8,128)(2,1)S(1)} %get-tuple-element.17.refs_0_.refs_4_, bf16[256,1536]{1,0:T(8,128)(2,1)S(1)} %collective-permute-done.6.refs_1_, bf16[1536,1536]{1,0:T(8,128)(2,1)S(1)} %staged.1.refs_8_.refs_2_, ...), custom_call_target="tpu_custom_call" | custom-call | flops 24159192 | bytes 1024 | tf_op jit(solution)/shard_map/partial_products/pallas_call | solution.py:72
  42.8 0.0 collective-permute-done.12.refs_1_
  42.8 0.2 collective-permute-start.14
  43.0 0.3 collective-permute-start.11
  43.3 5.3 %partial_products.5 = (f32[128,1536]{1,0:T(8,128)S(1)}, bf16[128,1536]{1,0:T(8,128)(2,1)S(1)}) custom-call(bf16[256,1536]{1,0:T(8,128)(2,1)S(1)} %get-tuple-element.17.refs_0_.refs_4_, bf16[256,1536]{1,0:T(8,128)(2,1)S(1)} %collective-permute-done.6.refs_1_, bf16[6144,1536]{1,0:T(8,128)(2,1)} %refs_2_.5, bf16[6144,1536]{1,0:T(8,128)(2,1)} %collective-permute-done.7.refs_3_, ...), custom_call_target="tpu_custom_call" | custom-call | flops 24159192 | bytes 1024 | tf_op jit(solution)/shard_map/partial_products/pallas_call | solution.py:72
  48.6 1.8 %collective-permute-start.10 = (bf16[128,1536]{1,0:T(8,128)(2,1)S(1)}, bf16[128,1536]{1,0:T(8,128)(2,1)S(1)}, u32[]{:S(2)}, u32[]{:S(2)}) collective-permute-start(bf16[128,1536]{1,0:T(8,128)(2,1)S(1)} %get-tuple-element.25), channel_id=1, source_target_pairs={{0,2},{2,0},{1,3},{3,1},{4,6},{6,4},{5,7},{7,5},{8,10},{10,8},{9,1... | collective-permute-start | bytes 1179656 | tf_op jit(solution)/shard_map/ppermute | solution.py:38
  50.4 5.3 %partial_products.6 = (f32[128,1536]{1,0:T(8,128)S(1)}, bf16[128,1536]{1,0:T(8,128)(2,1)S(1)}) custom-call(bf16[256,1536]{1,0:T(8,128)(2,1)S(1)} %get-tuple-element.17.refs_0_.refs_4_, bf16[256,1536]{1,0:T(8,128)(2,1)S(1)} %collective-permute-done.6.refs_1_, bf16[6144,1536]{1,0:T(8,128)(2,1)} %refs_2_.5, bf16[6144,1536]{1,0:T(8,128)(2,1)} %collective-permute-done.7.refs_3_, ...), custom_call_target="tpu_custom_call" | custom-call | flops 24159192 | bytes 1024 | tf_op jit(solution)/shard_map/partial_products/pallas_call | solution.py:72
  55.7 0.3 collective-permute-start.9
  56.1 5.3 %partial_products.7 = (f32[128,1536]{1,0:T(8,128)S(1)}, bf16[128,1536]{1,0:T(8,128)(2,1)S(1)}) custom-call(bf16[256,1536]{1,0:T(8,128)(2,1)S(1)} %get-tuple-element.17.refs_0_.refs_4_, bf16[256,1536]{1,0:T(8,128)(2,1)S(1)} %collective-permute-done.6.refs_1_, bf16[6144,1536]{1,0:T(8,128)(2,1)} %refs_2_.5, bf16[6144,1536]{1,0:T(8,128)(2,1)} %collective-permute-done.7.refs_3_, ...), custom_call_target="tpu_custom_call" | custom-call | flops 24159192 | bytes 1024 | tf_op jit(solution)/shard_map/partial_products/pallas_call | solution.py:72
  61.4 0.0 collective-permute-done.13.refs_2_
  61.4 1.8 %collective-permute-start.8 = (bf16[128,1536]{1,0:T(8,128)(2,1)S(1)}, bf16[128,1536]{1,0:T(8,128)(2,1)S(1)}, u32[]{:S(2)}, u32[]{:S(2)}) collective-permute-start(bf16[128,1536]{1,0:T(8,128)(2,1)S(1)} %get-tuple-element.23), channel_id=1, source_target_pairs={{0,2},{2,0},{1,3},{3,1},{4,6},{6,4},{5,7},{7,5},{8,10},{10,8},{9,1... | collective-permute-start | bytes 1179656 | tf_op jit(solution)/shard_map/ppermute | solution.py:38
  63.2 0.0 collective-permute-done.14.refs_3_
  63.2 13.5 %weight_products.1.refs_3_ = bf16[6144,1536]{1,0:T(8,128)(2,1)} custom-call(bf16[128,6144]{1,0:T(8,128)(2,1)S(1)} %hidden_part.1.refs_1_.refs_0_, bf16[128,6144]{1,0:T(8,128)(2,1)S(1)} %collective-permute-done.12.refs_1_, bf16[128,6144]{1,0:T(8,128)(2,1)S(1)} %collective-permute-done.13.refs_2_, bf16[128,6144]{1,0:T(8,128)(2,1)S(1)} %collective-permute-done.14.refs_3_, ...), custom_call_target="tpu_custom_call" | custom-call | flops 1024 | bytes 1024 | tf_op jit(solution)/shard_map/weight_products/pallas_call | solution.py:72
  76.8 0.0 collective-permute-done.11.refs_2_
  76.8 0.8 %last_step.4.refs_3_ = bf16[128,6144]{1,0:T(8,128)(2,1)} custom-call(f32[128,6144]{1,0:T(8,128)S(1)} %slopes.1.refs_1_.refs_0_, f32[128,1536]{1,0:T(8,128)S(1)} %get-tuple-element.19.refs_4_.refs_1_, bf16[128,1536]{1,0:T(8,128)(2,1)S(1)} %collective-permute-done.11.refs_2_, bf16[6144,1536]{1,0:T(8,128)(2,1)} %weight_products.1.refs_3_), custom_call_target="tpu_custom_call" | custom-call | flops 161061280 | bytes 1024 | tf_op jit(solution)/shard_map/last_step/pallas_call | solution.py:72
  77.6 0.0 collective-permute-done.10.refs_2_
  77.6 0.8 %last_step.5.refs_3_ = bf16[128,6144]{1,0:T(8,128)(2,1)} custom-call(f32[128,6144]{1,0:T(8,128)S(1)} %slopes.1.refs_1_.refs_0_, f32[128,1536]{1,0:T(8,128)S(1)} %get-tuple-element.20.refs_4_.refs_1_, bf16[128,1536]{1,0:T(8,128)(2,1)S(1)} %collective-permute-done.10.refs_2_, bf16[128,6144]{1,0:T(8,128)(2,1)} %last_step.4.refs_3_), custom_call_target="tpu_custom_call", output_to_operand_aliasing={{}: (3, {})} | custom-call | flops 161061280 | bytes 1024 | tf_op jit(solution)/shard_map/last_step/pallas_call | solution.py:72
  78.4 0.0 collective-permute-done.9.refs_2_
  78.4 0.8 %last_step.6.refs_3_ = bf16[128,6144]{1,0:T(8,128)(2,1)} custom-call(f32[128,6144]{1,0:T(8,128)S(1)} %slopes.1.refs_1_.refs_0_, f32[128,1536]{1,0:T(8,128)S(1)} %get-tuple-element.21.refs_4_.refs_1_, bf16[128,1536]{1,0:T(8,128)(2,1)S(1)} %collective-permute-done.9.refs_2_, bf16[128,6144]{1,0:T(8,128)(2,1)} %last_step.5.refs_3_), custom_call_target="tpu_custom_call", output_to_operand_aliasing={{}: (3, {})} | custom-call | flops 161061280 | bytes 1024 | tf_op jit(solution)/shard_map/last_step/pallas_call | solution.py:72
  79.3 0.4 collective-permute-done.8.refs_2_
  79.7 0.8 %last_step.7 = bf16[128,6144]{1,0:T(8,128)(2,1)} custom-call(f32[128,6144]{1,0:T(8,128)S(1)} %slopes.1.refs_1_.refs_0_, f32[128,1536]{1,0:T(8,128)S(1)} %get-tuple-element.22.refs_6_.refs_1_, bf16[128,1536]{1,0:T(8,128)(2,1)S(1)} %collective-permute-done.8.refs_2_, bf16[128,6144]{1,0:T(8,128)(2,1)} %last_step.6.refs_3_), custom_call_target="tpu_custom_call", output_to_operand_aliasing={{}: (3, {})} | custom-call | flops 161061280 | bytes 1024 | tf_op jit(solution)/shard_map/last_step/pallas_call | solution.py:72
  (1 shorter events, 0.0 us)
Async XLA Ops:
  0.6 37.6 %collective-permute-start.7 = (bf16[6144,1536]{1,0:T(8,128)(2,1)}, bf16[6144,1536]{1,0:T(8,128)(2,1)}, u32[]{:S(2)}, u32[]{:S(2)}) collective-permute-start(bf16[6144,1536]{1,0:T(8,128)(2,1)} %refs_2_.5), channel_id=1, source_target_pairs={{1,0},{0,1},{3,2},{2,3},{5,4},{4,5},{7,6},{6,7},{9,8},{8,9},{11,10... | collective-permute-start | bytes 56623112 | tf_op jit(solution)/shard_map/ppermute | solution.py:42
  1.1 41.7 %collective-permute-start.12 = (bf16[128,6144]{1,0:T(8,128)(2,1)}, bf16[128,6144]{1,0:T(8,128)(2,1)S(1)}, u32[]{:S(2)}, u32[]{:S(2)}) collective-permute-start(bf16[128,6144]{1,0:T(8,128)(2,1)} %refs_0_.6), channel_id=1, source_target_pairs={{2,0},{0,2},{3,1},{1,3},{6,4},{4,6},{7,5},{5,7},{10,8},{8,10},{11,... | collective-permute-start | bytes 4718600 | tf_op jit(solution)/shard_map/ppermute | solution.py:42
  3.7 1.0 %copy-start.1 = (bf16[128,1536]{1,0:T(8,128)(2,1)S(1)}, bf16[128,1536]{1,0:T(8,128)(2,1)}, u32[]{:S(2)}) copy-start(bf16[128,1536]{1,0:T(8,128)(2,1)} %refs_0_.4) | copy-start | bytes 1179652
  4.7 9.6 %collective-permute-start = (bf16[64,1536]{1,0:T(8,128)(2,1)S(1)}, bf16[64,1536]{1,0:T(8,128)(2,1)S(1)}, u32[]{:S(2)}, u32[]{:S(2)}) collective-permute-start(bf16[64,1536]{1,0:T(8,128)(2,1)S(1)} %get-tuple-element.15.refs_1_.refs_0_), channel_id=1, source_target_pairs={{0,4},{4,8},{8,12},{12,0},{1,5},{5,9},{9,13},{13,1},{2,6},{6,10},{... | collective-permute-start | bytes 589832 | tf_op jit(solution)/shard_map/ppermute | solution.py:38
  6.4 11.8 %collective-permute-start.3 = (bf16[64,1536]{1,0:T(8,128)(2,1)S(1)}, bf16[64,1536]{1,0:T(8,128)(2,1)S(1)}, u32[]{:S(2)}, u32[]{:S(2)}) collective-permute-start(bf16[64,1536]{1,0:T(8,128)(2,1)S(1)} %get-tuple-element.16.refs_4_), channel_id=1, source_target_pairs={{0,4},{4,8},{8,12},{12,0},{1,5},{5,9},{9,13},{13,1},{2,6},{6,10},{... | collective-permute-start | bytes 589832 | tf_op jit(solution)/shard_map/ppermute | solution.py:38
  14.3 8.1 %collective-permute-start.1 = (bf16[64,1536]{1,0:T(8,128)(2,1)S(1)}, bf16[64,1536]{1,0:T(8,128)(2,1)S(1)}, u32[]{:S(2)}, u32[]{:S(2)}) collective-permute-start(bf16[64,1536]{1,0:T(8,128)(2,1)S(1)} %collective-permute-done.refs_1_), channel_id=1, source_target_pairs={{0,4},{4,8},{8,12},{12,0},{1,5},{5,9},{9,13},{13,1},{2,6},{6,10},{... | collective-permute-start | bytes 589832 | tf_op jit(solution)/shard_map/ppermute | solution.py:38
  18.2 9.6 %collective-permute-start.4 = (bf16[64,1536]{1,0:T(8,128)(2,1)S(1)}, bf16[64,1536]{1,0:T(8,128)(2,1)S(1)}, u32[]{:S(2)}, u32[]{:S(2)}) collective-permute-start(bf16[64,1536]{1,0:T(8,128)(2,1)S(1)} %collective-permute-done.3.refs_5_), channel_id=1, source_target_pairs={{0,4},{4,8},{8,12},{12,0},{1,5},{5,9},{9,13},{13,1},{2,6},{6,10},{... | collective-permute-start | bytes 589832 | tf_op jit(solution)/shard_map/ppermute | solution.py:38
  22.4 13.2 %collective-permute-start.2 = (bf16[64,1536]{1,0:T(8,128)(2,1)S(1)}, bf16[64,1536]{1,0:T(8,128)(2,1)S(1)}, u32[]{:S(2)}, u32[]{:S(2)}) collective-permute-start(bf16[64,1536]{1,0:T(8,128)(2,1)S(1)} %collective-permute-done.1.refs_2_), channel_id=1, source_target_pairs={{0,4},{4,8},{8,12},{12,0},{1,5},{5,9},{9,13},{13,1},{2,6},{6,10},{... | collective-permute-start | bytes 589832 | tf_op jit(solution)/shard_map/ppermute | solution.py:38
  27.8 7.8 %collective-permute-start.5 = (bf16[64,1536]{1,0:T(8,128)(2,1)S(1)}, bf16[64,1536]{1,0:T(8,128)(2,1)S(1)}, u32[]{:S(2)}, u32[]{:S(2)}) collective-permute-start(bf16[64,1536]{1,0:T(8,128)(2,1)S(1)} %collective-permute-done.4.refs_6_), channel_id=1, source_target_pairs={{0,4},{4,8},{8,12},{12,0},{1,5},{5,9},{9,13},{13,1},{2,6},{6,10},{... | collective-permute-start | bytes 589832 | tf_op jit(solution)/shard_map/ppermute | solution.py:38
  27.8 1.4 %copy-start = (bf16[128,6144]{1,0:T(8,128)(2,1)S(1)}, bf16[128,6144]{1,0:T(8,128)(2,1)}, u32[]{:S(2)}) copy-start(bf16[128,6144]{1,0:T(8,128)(2,1)} %refs_0_.6) | copy-start | bytes 4718596
  35.9 2.4 %collective-permute-start.6 = (bf16[256,1536]{1,0:T(8,128)(2,1)S(1)}, bf16[256,1536]{1,0:T(8,128)(2,1)S(1)}, u32[]{:S(2)}, u32[]{:S(2)}) collective-permute-start(bf16[256,1536]{1,0:T(8,128)(2,1)S(1)} %get-tuple-element.18.refs_5_), channel_id=1, source_target_pairs={{0,1},{1,0},{2,3},{3,2},{4,5},{5,4},{6,7},{7,6},{8,9},{9,8},{10,11... | collective-permute-start | bytes 2359304 | tf_op jit(solution)/shard_map/ppermute | solution.py:38
  36.0 25.4 %collective-permute-start.13 = (bf16[128,6144]{1,0:T(8,128)(2,1)S(1)}, bf16[128,6144]{1,0:T(8,128)(2,1)S(1)}, u32[]{:S(2)}, u32[]{:S(2)}) collective-permute-start(bf16[128,6144]{1,0:T(8,128)(2,1)S(1)} %hidden_part.1.refs_1_.refs_0_), channel_id=1, source_target_pairs={{1,0},{0,1},{3,2},{2,3},{5,4},{4,5},{7,6},{6,7},{9,8},{8,9},{11,10... | collective-permute-start | bytes 4718600 | tf_op jit(solution)/shard_map/ppermute | solution.py:42
  42.8 20.4 %collective-permute-start.14 = (bf16[128,6144]{1,0:T(8,128)(2,1)S(1)}, bf16[128,6144]{1,0:T(8,128)(2,1)S(1)}, u32[]{:S(2)}, u32[]{:S(2)}) collective-permute-start(bf16[128,6144]{1,0:T(8,128)(2,1)S(1)} %collective-permute-done.12.refs_1_), channel_id=1, source_target_pairs={{1,0},{0,1},{3,2},{2,3},{5,4},{4,5},{7,6},{6,7},{9,8},{8,9},{11,10... | collective-permute-start | bytes 4718600 | tf_op jit(solution)/shard_map/ppermute | solution.py:42
  43.0 33.7 %collective-permute-start.11 = (bf16[128,1536]{1,0:T(8,128)(2,1)S(1)}, bf16[128,1536]{1,0:T(8,128)(2,1)S(1)}, u32[]{:S(2)}, u32[]{:S(2)}) collective-permute-start(bf16[128,1536]{1,0:T(8,128)(2,1)S(1)} %get-tuple-element.26), channel_id=1, source_target_pairs={{0,2},{2,0},{1,3},{3,1},{4,6},{6,4},{5,7},{7,5},{8,10},{10,8},{9,1... | collective-permute-start | bytes 1179656 | tf_op jit(solution)/shard_map/ppermute | solution.py:38
  48.6 29.0 %collective-permute-start.10 = (bf16[128,1536]{1,0:T(8,128)(2,1)S(1)}, bf16[128,1536]{1,0:T(8,128)(2,1)S(1)}, u32[]{:S(2)}, u32[]{:S(2)}) collective-permute-start(bf16[128,1536]{1,0:T(8,128)(2,1)S(1)} %get-tuple-element.25), channel_id=1, source_target_pairs={{0,2},{2,0},{1,3},{3,1},{4,6},{6,4},{5,7},{7,5},{8,10},{10,8},{9,1... | collective-permute-start | bytes 1179656 | tf_op jit(solution)/shard_map/ppermute | solution.py:38
  55.7 22.7 %collective-permute-start.9 = (bf16[128,1536]{1,0:T(8,128)(2,1)S(1)}, bf16[128,1536]{1,0:T(8,128)(2,1)S(1)}, u32[]{:S(2)}, u32[]{:S(2)}) collective-permute-start(bf16[128,1536]{1,0:T(8,128)(2,1)S(1)} %get-tuple-element.24), channel_id=1, source_target_pairs={{0,2},{2,0},{1,3},{3,1},{4,6},{6,4},{5,7},{7,5},{8,10},{10,8},{9,1... | collective-permute-start | bytes 1179656 | tf_op jit(solution)/shard_map/ppermute | solution.py:38
  61.4 18.3 %collective-permute-start.8 = (bf16[128,1536]{1,0:T(8,128)(2,1)S(1)}, bf16[128,1536]{1,0:T(8,128)(2,1)S(1)}, u32[]{:S(2)}, u32[]{:S(2)}) collective-permute-start(bf16[128,1536]{1,0:T(8,128)(2,1)S(1)} %get-tuple-element.23), channel_id=1, source_target_pairs={{0,2},{2,0},{1,3},{3,1},{4,6},{6,4},{5,7},{7,5},{8,10},{10,8},{9,1... | collective-permute-start | bytes 1179656 | tf_op jit(solution)/shard_map/ppermute | solution.py:38
